TPU v7x, 128 devices: a whole 4x4x4 slice. The times are simulated.
128 devices in a mesh: dev: 128 (over z, x, y, core).
Axes of the slice: x: 4, y: 4, z: 4, core: 2. Of those that a mesh axis runs over, the one named last changes fastest.
Arguments:
- context: bfloat16 [80, 32768], P(None, 'dev'), may hold values from -6 to 6
- depth_logits: bfloat16 [118, 32768], P(None, 'dev'), may hold values from -256 to 256
- send_point: int32 [128, 128, 128], P('dev'), may hold values from -1 to 30207, as said below
- recv_cell: int32 [128, 128, 128], P('dev'), may hold values from -1 to 8191, as said below
- neighbour: int32 [128, 2, 8], P('dev'), may hold values from -1 to 1, as said below
- conv1_weight: bfloat16 [80, 720], replicated, may hold values from -0.21875 to 0.21875
- layer_scale: float32 [80], replicated, may hold values from 32 to 128
- layer_bias: float32 [80], replicated, may hold values from -3 to 3
- conv2_weight: bfloat16 [80, 720], replicated, may hold values from -0.21875 to 0.21875
- out_bias: float32 [80], replicated, may hold values from -3 to 3
Outputs:
- bev_out: float32 [128, 2, 80, 4096], P('dev')
Inputs may be any that keep to these rules, and one draw needn't show every extreme that they name: send_point holds -1 or a point of the source device as depth bin times 256 plus pixel; each point stands in at most one slot of its device; in every bucket of 128 slots the used slots come first; some destination receives 128 used slots from every source. recv_cell[t, s, k] is -1 exactly where send_point[s, t, k] is -1, else a cell of tile row t, tile times 4096 plus cell. The neighbour lists come from one grid of tiles in which row t holds 2 active tiles.
All inputs are finite; a program needn't handle non-finite values.
Results may differ from a plain program's by a relative error of at most 0.0045.
Values may be sent and summed in bfloat16 or wider, within the bound.
No kernel may reach another device: no remote copies, remote signals or barrier semaphores. Data moves between devices by JAX's collectives and lax.ppermute only.
A program may use at most 64 MiB of HBM per device.

v0:
```python
import functools

import jax
import jax.numpy as jnp
from jax import lax
from jax.experimental import pallas as pl
from jax.experimental.pallas import tpu as pltpu
from jax.sharding import PartitionSpec as P

SIDE = 64
CELLS = SIDE * SIDE
BF = jnp.bfloat16
F32 = jnp.float32
VMEM = pl.BlockSpec(memory_space=pltpu.VMEM)
SMEM = pl.BlockSpec(memory_space=pltpu.SMEM)


def params(megabytes):
    return pltpu.CompilerParams(vmem_limit_bytes=megabytes * 1024 * 1024)


def float_iota(shape, axis):
    return lax.broadcasted_iota(jnp.int32, shape, axis).astype(F32).astype(BF)


def lift_kernel(unroll, context, logits, send, out, wide, table):
    channels, pixels = context.shape
    depths = logits.shape[0]
    slots = send.shape[1]
    wide[...] = jnp.full(wide.shape, -1e30, F32)
    wide[0:depths, :] = logits[...].astype(F32)
    shifted = wide[...] - jnp.max(wide[...], axis=0, keepdims=True)
    powers = jnp.exp(shifted)
    prob = powers / jnp.sum(powers, axis=0, keepdims=True)
    high = prob.astype(BF)
    bins = wide.shape[0]
    table[0:channels, :] = context[...]
    table[channels : channels + bins, :] = high
    table[channels + bins : channels + 2 * bins, :] = (prob - high.astype(F32)).astype(BF)
    pixel_iota = float_iota((pixels, slots), 0)
    bin_iota = lax.broadcasted_iota(jnp.int32, (bins, slots), 0)
    one, zero = jnp.ones((), BF), jnp.zeros((), BF)

    def step(i, carry):
        points = [send[pl.ds(i * unroll + u, 1), :] for u in range(unroll)]
        picks = []
        for point in points:
            pixel = (point & (pixels - 1)).astype(F32).astype(BF)
            picks.append(jnp.where(pixel_iota == pixel, one, zero))
        found = jnp.dot(table[...], jnp.concatenate(picks, axis=1), preferred_element_type=F32)
        for u, point in enumerate(points):
            mine = found[:, u * slots : (u + 1) * slots]
            columns = mine[0:channels]
            probs = mine[channels : channels + bins] + mine[channels + bins :]
            chosen = jnp.where(bin_iota == (point >> 8), probs, 0.0)
            weight = jnp.sum(chosen, axis=0, keepdims=True)
            out[i * unroll + u] = (columns * weight).astype(BF)
        return carry

    lax.fori_loop(0, send.shape[0] // unroll, step, 0)


def lift(context, logits, send):
    channels, pixels = context.shape
    return pl.pallas_call(
        functools.partial(lift_kernel, 4),
        out_shape=jax.ShapeDtypeStruct((send.shape[0], channels, send.shape[1]), BF),
        in_specs=[VMEM] * 3,
        out_specs=VMEM,
        scratch_shapes=[pltpu.VMEM((128, pixels), F32), pltpu.VMEM((channels + 256, pixels), BF)],
        compiler_params=params(32),
    )(context, logits, send)


def pack_edges(top0, top1, bottom0, bottom1):
    lower = lax.broadcasted_iota(jnp.int32, top0.shape, 1) < SIDE
    top = jnp.where(lower, top0, pltpu.roll(top1, SIDE, 1))
    bottom = jnp.where(lower, pltpu.roll(bottom1, SIDE, 1), bottom0)
    return top.astype(BF), bottom.astype(BF)


def field_edges(field, tops, bottoms):
    parts = []
    for start in (0, CELLS, CELLS - 128, 2 * CELLS - 128):
        parts.append(field[:, start : start + 128].astype(F32))
    top, bottom = pack_edges(*parts)
    tops[...] = top
    bottoms[...] = bottom


def splat_kernel(groups, unroll, arrived, cells, bev, tops, bottoms, total):
    channels, slots = arrived.shape[1:]
    width = total.shape[1]
    shift = width.bit_length() - 1
    block = 256
    total[...] = jnp.zeros(total.shape, F32)
    cell_iota = float_iota((block, slots * unroll), 0)
    one, zero = jnp.ones((), BF), jnp.zeros((), BF)

    def step(i, carry):
        values = jnp.concatenate([arrived[i * unroll + u] for u in range(unroll)], axis=1)
        targets = jnp.concatenate([cells[pl.ds(i * unroll + u, 1), :] for u in range(unroll)], axis=1)
        group = targets >> shift
        place = targets & (width - 1)
        masked = []
        for g in range(groups):
            masked.append(values * jnp.where(group == g, 1.0, 0.0).astype(BF))
        grouped = jnp.concatenate(masked, axis=0)
        for j in range(width // block):
            spot = (place - j * block).astype(F32).astype(BF)
            pick = jnp.where(cell_iota == spot, one, zero)
            total[:, j * block : (j + 1) * block] += lax.dot_general(
                grouped, pick, (((1,), (1,)), ((), ())), preferred_element_type=F32
            )
        return carry

    lax.fori_loop(0, arrived.shape[0] // unroll, step, 0)
    for g in range(groups):
        bev[:, g * width : (g + 1) * width] = total[g * channels : (g + 1) * channels, :].astype(BF)
    field_edges(bev, tops, bottoms)


def splat(arrived, cells):
    channels = arrived.shape[1]
    groups = 4
    width = 2 * CELLS // groups
    edge = jax.ShapeDtypeStruct((channels, 128), BF)
    return pl.pallas_call(
        functools.partial(splat_kernel, groups, 8),
        out_shape=(jax.ShapeDtypeStruct((channels, 2 * CELLS), BF), edge, edge),
        in_specs=[VMEM] * 2,
        out_specs=(VMEM,) * 3,
        scratch_shapes=[pltpu.VMEM((groups * channels, width), F32)],
        compiler_params=params(32),
    )(arrived, cells)


def halo_images(above, below, links, tile):
    lane = lax.broadcasted_iota(jnp.int32, above.shape, 1)
    lower = lane < SIDE
    column = lane & (SIDE - 1)
    above_other = pltpu.roll(above, SIDE, 1)
    below_other = pltpu.roll(below, SIDE, 1)

    def pick(up, down):
        def gate(n, want):
            return jnp.where(links[tile, n] == want, 1.0, 0.0)

        high = above * gate(up, 0) + above_other * gate(up, 1)
        low = below * gate(down, 0) + below_other * gate(down, 1)
        return jnp.where(lower, low, high)

    west, center, east = pick(0, 5), pick(1, 6), pick(2, 7)
    left = jnp.where(column == 0, pltpu.roll(west, SIDE + 1, 1), pltpu.roll(center, 1, 1))
    right = jnp.where(column == SIDE - 1, pltpu.roll(east, SIDE - 1, 1), pltpu.roll(center, 127, 1))
    return left, center, right


def conv_tile(field, above, below, links, weight, tile, stack, product, finish):
    channels = field.shape[0]
    rows = 16
    shape = (rows, CELLS)
    column = lax.broadcasted_iota(jnp.int32, shape, 1) & (SIDE - 1)
    adjacent = jnp.where(links[tile, 3 if tile else 4] >= 0, 1.0, 0.0)

    def stack_rows(r, carry):
        at = pl.ds(pl.multiple_of(r * rows, rows), rows)
        mine = field[at, tile * CELLS : (tile + 1) * CELLS].astype(F32)
        other = field[at, (1 - tile) * CELLS : (2 - tile) * CELLS].astype(F32) * adjacent
        if tile:
            left_edge, right_edge = pltpu.roll(other, CELLS - SIDE + 1, 1), 0.0
        else:
            left_edge, right_edge = 0.0, pltpu.roll(other, SIDE - 1, 1)
        left = jnp.where(column == 0, left_edge, pltpu.roll(mine, 1, 1))
        right = jnp.where(column == SIDE - 1, right_edge, pltpu.roll(mine, CELLS - 1, 1))
        for b, image in enumerate((left, mine, right)):
            to = pl.ds(pl.multiple_of(b * channels + r * rows, rows), rows)
            stack[to, 0:CELLS] = image.astype(BF)
        return carry

    lax.fori_loop(0, channels // rows, stack_rows, 0)
    images = halo_images(above[...].astype(F32), below[...].astype(F32), links, tile)
    for b, image in enumerate(images):
        stack[b * channels : (b + 1) * channels, CELLS : CELLS + 128] = image.astype(BF)
    span = CELLS + 128
    for start in range(0, span, 512):
        stop = min(start + 512, span)
        product[:, start:stop] = jnp.dot(
            weight[...], stack[:, start:stop], preferred_element_type=F32
        )

    def sum_rows(r, carry):
        def part(a):
            return product[pl.ds(pl.multiple_of(a * channels + r * rows, rows), rows), :]

        below_part = part(2)
        outer = part(0) + jnp.concatenate([below_part[:, 128:], below_part[:, 0:128]], axis=1)
        summed = part(1)[:, 0:CELLS] + pltpu.roll(outer, SIDE, 1)[:, 0:CELLS]
        finish(tile, pl.ds(pl.multiple_of(r * rows, rows), rows), summed)
        return carry

    lax.fori_loop(0, channels // rows, sum_rows, 0)


def first_kernel(field, above, below, links, weight, scale, bias, hidden, tops, bottoms, stack, product):
    def finish(tile, at, summed):
        active = jnp.maximum(scale[at, :] * summed + bias[at, :], 0.0)
        hidden[at, tile * CELLS : (tile + 1) * CELLS] = active.astype(BF)

    for tile in range(2):
        conv_tile(field, above, below, links, weight, tile, stack, product, finish)
    field_edges(hidden, tops, bottoms)


def second_kernel(field, above, below, links, weight, bias, out, stack, product):
    def finish(tile, at, summed):
        out[tile, at, :] = summed + bias[at, :]

    for tile in range(2):
        conv_tile(field, above, below, links, weight, tile, stack, product, finish)


def conv_scratch(channels):
    return [
        pltpu.VMEM((3 * channels, CELLS + 128), BF),
        pltpu.VMEM((3 * channels, CELLS + 128), F32),
    ]


def first_conv(field, above, below, links, weight, scale, bias):
    channels = field.shape[0]
    edge = jax.ShapeDtypeStruct((channels, 128), BF)
    return pl.pallas_call(
        first_kernel,
        out_shape=(jax.ShapeDtypeStruct(field.shape, BF), edge, edge),
        in_specs=[VMEM, VMEM, VMEM, SMEM, VMEM, VMEM, VMEM],
        out_specs=(VMEM,) * 3,
        scratch_shapes=conv_scratch(channels),
        compiler_params=params(32),
    )(field, above, below, links, weight, scale, bias)


def second_conv(field, above, below, links, weight, bias):
    channels = field.shape[0]
    return pl.pallas_call(
        second_kernel,
        out_shape=jax.ShapeDtypeStruct((2, channels, CELLS), F32),
        in_specs=[VMEM, VMEM, VMEM, SMEM, VMEM, VMEM],
        out_specs=VMEM,
        scratch_shapes=conv_scratch(channels),
        compiler_params=params(32),
    )(field, above, below, links, weight, bias)


def exchange(tops, bottoms):
    devices = lax.axis_size("dev")
    above = lax.ppermute(bottoms, "dev", [(i, i + 1) for i in range(devices - 1)])
    below = lax.ppermute(tops, "dev", [(i + 1, i) for i in range(devices - 1)])
    return above, below


def by_row_tap(weight):
    channels = weight.shape[0]
    return weight.reshape(channels, 3, 3 * channels).transpose(1, 0, 2).reshape(3 * channels, -1)


def per_device(
    context,
    depth_logits,
    send_point,
    recv_cell,
    neighbour,
    conv1_weight,
    layer_scale,
    layer_bias,
    conv2_weight,
    out_bias,
):
    lifted = lift(context, depth_logits, send_point[0])
    arrived = lax.all_to_all(lifted, "dev", split_axis=0, concat_axis=0, tiled=True)
    bev, tops, bottoms = splat(arrived, recv_cell[0])
    links = neighbour[0]
    above, below = exchange(tops, bottoms)
    hidden, tops, bottoms = first_conv(
        bev,
        above,
        below,
        links,
        by_row_tap(conv1_weight),
        layer_scale[:, None],
        layer_bias[:, None],
    )
    above, below = exchange(tops, bottoms)
    out = second_conv(hidden, above, below, links, by_row_tap(conv2_weight), out_bias[:, None])
    return out[None]


def solution(mesh):
    in_specs = (
        P(None, "dev"),
        P(None, "dev"),
        P("dev", None, None),
        P("dev", None, None),
        P("dev", None, None),
        P(),
        P(),
        P(),
        P(),
        P(),
    )
    out_specs = P("dev", None, None, None)
    return jax.shard_map(
        per_device, mesh=mesh, in_specs=in_specs, out_specs=out_specs, check_vma=False
    )
```

profile of v0, /device:TPU:31, one launch (start us, length us, event | category | flops | bytes accessed | tf_op | source)
XLA Modules:
  0.0 119.3 jit_solution(9941384137761329595)
XLA Ops:
  0.0 0.0 copy-start
  0.0 0.8 copy-done
  0.8 0.8 copy-done.2
  1.7 0.8 copy-done.3
  2.4 8.9 %shard_map.100 = bf16[128,80,128]{2,1,0:T(8,128)(2,1)S(1)} custom-call(bf16[80,256]{1,0:T(8,128)(2,1)S(1)} %copy-done.3, bf16[118,256]{1,0:T(8,128)(2,1)S(1)} %copy-done.2, s32[128,128]{1,0:T(8,128)S(1)} %bitcast.13), custom_call_target="tpu_custom_call" | custom-call | tf_op jit(solution)/shard_map/pallas_call | solution.py:65
  11.3 0.0 copy-start.1
  11.3 41.9 %all_to_all.5.arrived = bf16[128,80,128]{2,1,0:T(8,128)(2,1)S(1)} all-to-all(bf16[128,80,128]{2,1,0:T(8,128)(2,1)S(1)} %shard_map.100), channel_id=1, replica_groups=mesh['dev'=128] {'dev'}, dimensions={0} | all-to-all | bytes 5242880 | tf_op jit(solution)/shard_map/all_to_all | solution.py:280
  53.3 0.0 copy-start.6
  53.3 0.0 copy-done.1
  53.3 0.0 copy-start.9
  53.3 25.2 %shard_map.101 = (bf16[80,8192]{1,0:T(8,128)(2,1)S(1)}, bf16[80,128]{1,0:T(8,128)(2,1)S(1)}, bf16[80,128]{1,0:T(8,128)(2,1)S(1)}) custom-call(bf16[128,80,128]{2,1,0:T(8,128)(2,1)S(1)} %all_to_all.5.arrived, s32[128,128]{1,0:T(8,128)S(1)} %bitcast.14), custom_call_target="tpu_custom_call" | custom-call | tf_op jit(solution)/shard_map/pallas_call | solution.py:128
  78.5 7.4 %collective-permute-start = (bf16[80,128]{1,0:T(8,128)(2,1)S(1)}, bf16[80,128]{1,0:T(8,128)(2,1)S(1)}, u32[]{:S(2)}, u32[]{:S(2)}) collective-permute-start(bf16[80,128]{1,0:T(8,128)(2,1)S(1)} %get-tuple-element.12), channel_id=1, source_target_pairs={{0,1},{1,2},{2,3},{3,4},{4,5},{5,6},{6,7},{7,8},{8,9},{9,10},{10,1... | collective-permute-start | bytes 61448 | tf_op jit(solution)/shard_map/ppermute | solution.py:257
  86.0 1.9 %collective-permute-start.1 = (bf16[80,128]{1,0:T(8,128)(2,1)S(1)}, bf16[80,128]{1,0:T(8,128)(2,1)S(1)}, u32[]{:S(2)}, u32[]{:S(2)}) collective-permute-start(bf16[80,128]{1,0:T(8,128)(2,1)S(1)} %get-tuple-element.13), channel_id=1, source_target_pairs={{1,0},{2,1},{3,2},{4,3},{5,4},{6,5},{7,6},{8,7},{9,8},{10,9},{11,1... | collective-permute-start | bytes 61448 | tf_op jit(solution)/shard_map/ppermute | solution.py:258
  87.9 0.0 copy-done.5
  87.9 0.2 reshape.12
  88.1 0.0 copy-done.7
  88.1 0.1 copy.17.scale
  88.2 0.0 copy-done.8
  88.2 0.1 copy.18.bias
  88.3 0.0 collective-permute-done.above
  88.3 7.0 %collective-permute-done.1.below = bf16[80,128]{1,0:T(8,128)(2,1)S(1)} collective-permute-done((bf16[80,128]{1,0:T(8,128)(2,1)S(1)}, bf16[80,128]{1,0:T(8,128)(2,1)S(1)}, u32[]{:S(2)}, u32[]{:S(2)}) %collective-permute-start.1) | collective-permute-done | bytes 20512 | tf_op jit(solution)/shard_map/ppermute | solution.py:258
  95.3 0.0 copy-done.4
  95.3 5.7 %shard_map.102 = (bf16[80,8192]{1,0:T(8,128)(2,1)S(1)}, bf16[80,128]{1,0:T(8,128)(2,1)S(1)}, bf16[80,128]{1,0:T(8,128)(2,1)S(1)}) custom-call(bf16[80,8192]{1,0:T(8,128)(2,1)S(1)} %get-tuple-element.11.field, bf16[80,128]{1,0:T(8,128)(2,1)S(1)} %collective-permute-done.above, bf16[80,128]{1,0:T(8,128)(2,1)S(1)} %collective-permute-done.1.below, ...), custom_call_target="tpu_custom_call" | custom-call | tf_op jit(solution)/shard_map/pallas_call | solution.py:233
  101.0 1.9 %collective-permute-start.2 = (bf16[80,128]{1,0:T(8,128)(2,1)S(1)}, bf16[80,128]{1,0:T(8,128)(2,1)S(1)}, u32[]{:S(2)}, u32[]{:S(2)}) collective-permute-start(bf16[80,128]{1,0:T(8,128)(2,1)S(1)} %get-tuple-element.15), channel_id=1, source_target_pairs={{0,1},{1,2},{2,3},{3,4},{4,5},{5,6},{6,7},{7,8},{8,9},{9,10},{10,1... | collective-permute-start | bytes 61448 | tf_op jit(solution)/shard_map/ppermute | solution.py:257
  103.0 2.4 %collective-permute-start.3 = (bf16[80,128]{1,0:T(8,128)(2,1)S(1)}, bf16[80,128]{1,0:T(8,128)(2,1)S(1)}, u32[]{:S(2)}, u32[]{:S(2)}) collective-permute-start(bf16[80,128]{1,0:T(8,128)(2,1)S(1)} %get-tuple-element.16), channel_id=1, source_target_pairs={{1,0},{2,1},{3,2},{4,3},{5,4},{6,5},{7,6},{8,7},{9,8},{10,9},{11,1... | collective-permute-start | bytes 61448 | tf_op jit(solution)/shard_map/ppermute | solution.py:258
  105.4 0.0 copy-done.6
  105.4 0.2 reshape.14
  105.6 0.0 copy-done.9
  105.6 0.1 copy.20.bias
  105.7 0.0 collective-permute-done.2.above
  105.7 6.6 %collective-permute-done.3.below = bf16[80,128]{1,0:T(8,128)(2,1)S(1)} collective-permute-done((bf16[80,128]{1,0:T(8,128)(2,1)S(1)}, bf16[80,128]{1,0:T(8,128)(2,1)S(1)}, u32[]{:S(2)}, u32[]{:S(2)}) %collective-permute-start.3) | collective-permute-done | bytes 20512 | tf_op jit(solution)/shard_map/ppermute | solution.py:258
  112.3 7.0 %shard_map.103 = f32[2,80,4096]{2,1,0:T(8,128)} custom-call(bf16[80,8192]{1,0:T(8,128)(2,1)S(1)} %get-tuple-element.14.field, bf16[80,128]{1,0:T(8,128)(2,1)S(1)} %collective-permute-done.2.above, bf16[80,128]{1,0:T(8,128)(2,1)S(1)} %collective-permute-done.3.below, s32[2,8]{1,0:T(2,128)S(1)} %bitcast.16, bf16[240,240]{1,0:T(8,128)(2,1)S(1)} %bitcast.11, ...), custom_call_target="tpu_custom_call" | custom-call | tf_op jit(solution)/shard_map/pallas_call | solution.py:245
  (8 shorter events, 0.0 us)
Async XLA Ops:
  0.0 0.8 copy-start
  0.8 0.8 copy-start.2
  1.7 0.8 copy-start.3
  11.3 41.9 %copy-start.1 = (s32[1,128,128]{2,1,0:T(8,128)S(1)}, s32[1,128,128]{2,1,0:T(8,128)}, u32[]{:S(2)}) copy-start(s32[1,128,128]{2,1,0:T(8,128)} %param.13) | copy-start | bytes 196612
  53.2 34.7 %copy-start.5 = (bf16[80,720]{1,0:T(8,128)(2,1)S(1)}, bf16[80,720]{1,0:T(8,128)(2,1)}, u32[]{:S(2)}) copy-start(bf16[80,720]{1,0:T(8,128)(2,1)} %param.15) | copy-start | bytes 345604
  53.3 34.9 %copy-start.7 = (f32[80]{0:T(128)S(1)}, f32[80]{0:T(128)}, u32[]{:S(2)}) copy-start(f32[80]{0:T(128)} %param.16) | copy-start | bytes 964
  53.3 35.0 %copy-start.8 = (f32[80]{0:T(128)S(1)}, f32[80]{0:T(128)}, u32[]{:S(2)}) copy-start(f32[80]{0:T(128)} %param.17) | copy-start | bytes 964
  53.3 42.0 %copy-start.4 = (s32[1,2,8]{2,1,0:T(2,128)S(1)}, s32[1,2,8]{2,1,0:T(2,128)}, u32[]{:S(2)}) copy-start(s32[1,2,8]{2,1,0:T(2,128)} %param.14) | copy-start | bytes 196
  53.3 52.1 %copy-start.6 = (bf16[80,720]{1,0:T(8,128)(2,1)S(1)}, bf16[80,720]{1,0:T(8,128)(2,1)}, u32[]{:S(2)}) copy-start(bf16[80,720]{1,0:T(8,128)(2,1)} %param.18) | copy-start | bytes 345604
  53.3 52.3 %copy-start.9 = (f32[80]{0:T(128)S(1)}, f32[80]{0:T(128)}, u32[]{:S(2)}) copy-start(f32[80]{0:T(128)} %param.19) | copy-start | bytes 964
  78.5 9.8 %collective-permute-start = (bf16[80,128]{1,0:T(8,128)(2,1)S(1)}, bf16[80,128]{1,0:T(8,128)(2,1)S(1)}, u32[]{:S(2)}, u32[]{:S(2)}) collective-permute-start(bf16[80,128]{1,0:T(8,128)(2,1)S(1)} %get-tuple-element.12), channel_id=1, source_target_pairs={{0,1},{1,2},{2,3},{3,4},{4,5},{5,6},{6,7},{7,8},{8,9},{9,10},{10,1... | collective-permute-start | bytes 61448 | tf_op jit(solution)/shard_map/ppermute | solution.py:257
  86.0 9.3 %collective-permute-start.1 = (bf16[80,128]{1,0:T(8,128)(2,1)S(1)}, bf16[80,128]{1,0:T(8,128)(2,1)S(1)}, u32[]{:S(2)}, u32[]{:S(2)}) collective-permute-start(bf16[80,128]{1,0:T(8,128)(2,1)S(1)} %get-tuple-element.13), channel_id=1, source_target_pairs={{1,0},{2,1},{3,2},{4,3},{5,4},{6,5},{7,6},{8,7},{9,8},{10,9},{11,1... | collective-permute-start | bytes 61448 | tf_op jit(solution)/shard_map/ppermute | solution.py:258
  101.0 4.7 %collective-permute-start.2 = (bf16[80,128]{1,0:T(8,128)(2,1)S(1)}, bf16[80,128]{1,0:T(8,128)(2,1)S(1)}, u32[]{:S(2)}, u32[]{:S(2)}) collective-permute-start(bf16[80,128]{1,0:T(8,128)(2,1)S(1)} %get-tuple-element.15), channel_id=1, source_target_pairs={{0,1},{1,2},{2,3},{3,4},{4,5},{5,6},{6,7},{7,8},{8,9},{9,10},{10,1... | collective-permute-start | bytes 61448 | tf_op jit(solution)/shard_map/ppermute | solution.py:257
  103.0 9.3 %collective-permute-start.3 = (bf16[80,128]{1,0:T(8,128)(2,1)S(1)}, bf16[80,128]{1,0:T(8,128)(2,1)S(1)}, u32[]{:S(2)}, u32[]{:S(2)}) collective-permute-start(bf16[80,128]{1,0:T(8,128)(2,1)S(1)} %get-tuple-element.16), channel_id=1, source_target_pairs={{1,0},{2,1},{3,2},{4,3},{5,4},{6,5},{7,6},{8,7},{9,8},{10,9},{11,1... | collective-permute-start | bytes 61448 | tf_op jit(solution)/shard_map/ppermute | solution.py:258
where the time goes:
time: 120 us; the launch traced here: 119 us
  Pallas kernels  46.8 us (39%)
  blocking collectives  41.9 us (35%)
  starting transfers between devices  13.7 us (11%)
  waiting for transfers between devices  13.6 us (11%)
  local copies, waits for them, and re-layouts  3.12 us (3%)
    all_to_all x1, blocking collectives, per_device(): lax.all_to_all(lifted, 'dev', split_axis=0, concat_axis=0, tiled=True)  41.9 us
    pallas_call x1, Pallas kernels, splat(): pl.pallas_call(functools.partial(splat_kernel, groups, 8), out_shape=(jax...  25.2 us
    ppermute x2, waiting for transfers between devices, exchange(): below = lax.ppermute(tops, 'dev', [(i + 1, i) for i in range(devices - 1)])  13.6 us
    ppermute x2, starting transfers between devices, exchange(): lax.ppermute(bottoms, 'dev', [(i, i + 1) for i in range(devices - 1)])  9.36 us
    pallas_call x1, Pallas kernels, lift(): pl.pallas_call(functools.partial(lift_kernel, 4), out_shape=jax.ShapeDtyp...  8.87 us
    pallas_call x1, Pallas kernels, second_conv(): pl.pallas_call(second_kernel, out_shape=jax.ShapeDtypeStruct((2, channels...  6.99 us
    pallas_call x1, Pallas kernels, first_conv(): pl.pallas_call(first_kernel, out_shape=(jax.ShapeDtypeStruct(field.shape,...  5.73 us
    ppermute x2, starting transfers between devices, exchange(): below = lax.ppermute(tops, 'dev', [(i + 1, i) for i in range(devices - 1)])  4.32 us
  transfers between devices with their start and end apart: 4, of which 2 were waited for; matrix products, arithmetic and copies ran while one was open for 1% of the time, Pallas kernels for 0%

commit v1 on v0

v1 whole, which is shorter than its diff:
```python
import functools

import jax
import jax.numpy as jnp
from jax import lax
from jax.experimental import pallas as pl
from jax.experimental.pallas import tpu as pltpu
from jax.sharding import PartitionSpec as P

SIDE = 64
PARTS = (80,)
CELLS = SIDE * SIDE
BF = jnp.bfloat16
F32 = jnp.float32
VMEM = pl.BlockSpec(memory_space=pltpu.VMEM)
SMEM = pl.BlockSpec(memory_space=pltpu.SMEM)


def params(megabytes):
    return pltpu.CompilerParams(vmem_limit_bytes=megabytes * 1024 * 1024)


def float_iota(shape, axis):
    return lax.broadcasted_iota(jnp.int32, shape, axis).astype(F32).astype(BF)


def split_high(value):
    high = value.astype(BF).astype(F32)
    return high, value - high


def lift_kernel(unroll, context, logits, send, *rest):
    *outs, wide, table = rest
    channels, pixels = context.shape
    depths = logits.shape[0]
    slots = send.shape[1]
    bins = -(-depths // 8) * 8
    values = logits[...].astype(F32)
    largest = jnp.max(values, axis=0, keepdims=True)
    inverse = 1.0 / jnp.sum(jnp.exp(values - largest), axis=0, keepdims=True)
    wide[...] = jnp.zeros(wide.shape, F32)
    wide[0:depths, :] = values
    wide[bins : bins + 1, :] = largest
    for n in range(3):
        high, inverse = split_high(inverse)
        wide[bins + 1 + n : bins + 2 + n, :] = high
    table[0:channels, :] = context[...]
    table[channels:, :] = wide[...].astype(BF)
    pixel_iota = float_iota((pixels, slots), 0)
    bin_iota = lax.broadcasted_iota(jnp.int32, (8, slots), 0)
    one, zero = jnp.ones((), BF), jnp.zeros((), BF)

    def step(i, carry):
        points = [send[pl.ds(i * unroll + u, 1), :] for u in range(unroll)]
        picks = []
        for point in points:
            pixel = (point & (pixels - 1)).astype(F32).astype(BF)
            picks.append(jnp.where(pixel_iota == pixel, one, zero))
        for v in range(0, unroll, 2):
            found = jnp.dot(
                table[...], jnp.concatenate(picks[v : v + 2], axis=1), preferred_element_type=F32
            )
            for u in (v, v + 1):
                point = points[u]
                mine = found[:, (u - v) * slots : (u - v + 1) * slots]
                offset = (point >> 8) - bin_iota
                chosen = jnp.zeros((8, slots), F32)
                for r in range(0, bins, 8):
                    chosen = jnp.where(offset == r, mine[channels + r : channels + r + 8], chosen)
                logit = jnp.sum(chosen, axis=0, keepdims=True)
                tail = mine[channels + bins :]
                scale = tail[1:2] + tail[2:3] + tail[3:4]
                weight = jnp.exp(logit - tail[0:1]) * scale
                weight = jnp.where(point >= 0, weight, 0.0)
                lifted = (mine[0:channels] * weight).astype(BF)
                first = 0
                for out in outs:
                    out[i * unroll + u] = lifted[first : first + out.shape[1]]
                    first += out.shape[1]
        return carry

    lax.fori_loop(0, send.shape[0] // unroll, step, 0)


def lift(context, logits, send):
    channels, pixels = context.shape
    return pl.pallas_call(
        functools.partial(lift_kernel, 32),
        out_shape=[jax.ShapeDtypeStruct((send.shape[0], part, send.shape[1]), BF) for part in PARTS],
        in_specs=[VMEM] * 3,
        out_specs=[VMEM] * len(PARTS),
        scratch_shapes=[pltpu.VMEM((128, pixels), F32), pltpu.VMEM((channels + 128, pixels), BF)],
        compiler_params=params(32),
    )(context, logits, send)


def field_edges(field, tops, bottoms):
    for j in range(2):
        at = slice(j * 128, (j + 1) * 128)
        tops[:, at] = field[:, j * CELLS : j * CELLS + 128]
        bottoms[:, at] = field[:, (j + 1) * CELLS - 128 : (j + 1) * CELLS]


def splat_kernel(groups, unroll, arrived, cells, *rest):
    *before, bev = rest[: len(rest) - 1 if len(rest) == 2 else len(rest) - 3]
    total = rest[-1]
    channels, slots = arrived.shape[1:]
    width = total.shape[1]
    shift = width.bit_length() - 1
    block = 256
    total[...] = jnp.zeros(total.shape, F32)
    cell_iota = float_iota((block, slots * unroll), 0)
    one, zero = jnp.ones((), BF), jnp.zeros((), BF)

    def step(i, carry):
        values = jnp.concatenate([arrived[i * unroll + u] for u in range(unroll)], axis=1)
        targets = jnp.concatenate([cells[pl.ds(i * unroll + u, 1), :] for u in range(unroll)], axis=1)
        group = targets >> shift
        place = targets & (width - 1)
        masked = []
        for g in range(groups):
            masked.append(values * jnp.where(group == g, 1.0, 0.0).astype(BF))
        grouped = jnp.concatenate(masked, axis=0)
        for j in range(width // block):
            spot = (place - j * block).astype(F32).astype(BF)
            pick = jnp.where(cell_iota == spot, one, zero)
            total[:, j * block : (j + 1) * block] += lax.dot_general(
                grouped, pick, (((1,), (1,)), ((), ())), preferred_element_type=F32
            )
        return carry

    lax.fori_loop(0, arrived.shape[0] // unroll, step, 0)
    first = bev.shape[0] - channels
    if before:
        bev[0:first, :] = before[0][...]
    for g in range(groups):
        bev[first:, g * width : (g + 1) * width] = total[g * channels : (g + 1) * channels, :].astype(BF)
    if len(rest) > 2:
        field_edges(bev, rest[-3], rest[-2])


def splat(arrived, cells, before=None, last=True):
    channels = arrived.shape[1]
    groups = 4
    while groups * channels < 256:
        groups *= 2
    width = 2 * CELLS // groups
    total = channels + (0 if before is None else before.shape[0])
    edge = jax.ShapeDtypeStruct((total, 256), BF)
    shapes = (jax.ShapeDtypeStruct((total, 2 * CELLS), BF),) + ((edge, edge) if last else ())
    operands = (arrived, cells) + (() if before is None else (before,))
    return pl.pallas_call(
        functools.partial(splat_kernel, groups, 32),
        out_shape=shapes,
        in_specs=[VMEM] * len(operands),
        out_specs=(VMEM,) * len(shapes),
        scratch_shapes=[pltpu.VMEM((groups * channels, width), F32)],
        compiler_params=params(32),
        cost_estimate=pl.CostEstimate(
            flops=2 * arrived.shape[0] * 128 * 2 * CELLS * channels,
            bytes_accessed=arrived.size * 2 + total * 2 * CELLS * 2,
            transcendentals=0,
        ),
    )(*operands)


def lane_images(center, west, east):
    column = lax.broadcasted_iota(jnp.int32, center.shape, 1) & (SIDE - 1)
    left = jnp.where(column == 0, pltpu.roll(west, SIDE + 1, 1), pltpu.roll(center, 1, 1))
    right = jnp.where(column == SIDE - 1, pltpu.roll(east, SIDE - 1, 1), pltpu.roll(center, 127, 1))
    return left, center, right


def halves(low, high):
    return jnp.where(lax.broadcasted_iota(jnp.int32, low.shape, 1) < SIDE, low, high)


def stack_tile(field, links, tile, stack):
    channels = field.shape[0]
    rows = 16
    column = lax.broadcasted_iota(jnp.int32, (rows, CELLS), 1) & (SIDE - 1)
    adjacent = jnp.where(links[tile, 3 if tile else 4] >= 0, 1.0, 0.0)
    for r in range(0, channels, rows):
        mine = field[r : r + rows, tile * CELLS : (tile + 1) * CELLS].astype(F32)
        other = field[r : r + rows, (1 - tile) * CELLS : (2 - tile) * CELLS].astype(F32) * adjacent
        west, east = 0.0, 0.0
        if tile:
            west = pltpu.roll(other, CELLS - SIDE + 1, 1)
        else:
            east = pltpu.roll(other, SIDE - 1, 1)
        left = jnp.where(column == 0, west, pltpu.roll(mine, 1, 1))
        right = jnp.where(column == SIDE - 1, east, pltpu.roll(mine, CELLS - 1, 1))
        stack[r : r + rows, 0:CELLS] = left.astype(BF)
        stack[channels + r : channels + r + rows, 0:CELLS] = field[
            r : r + rows, tile * CELLS : (tile + 1) * CELLS
        ]
        stack[2 * channels + r : 2 * channels + r + rows, 0:CELLS] = right.astype(BF)


def stack_lanes(stack, start, images):
    channels = images[0].shape[0]
    for b, image in enumerate(images):
        stack[b * channels : (b + 1) * channels, start : start + 128] = image.astype(BF)


def multiply(weight, stack, product):
    span = stack.shape[1]
    for start in range(0, span, 512):
        stop = min(start + 512, span)
        product[:, start:stop] = jnp.dot(
            weight[...], stack[:, start:stop], preferred_element_type=F32
        )


def sum_tile(product, finish):
    channels = product.shape[0] // 3
    rows = 16
    for r in range(0, channels, rows):

        def part(a):
            return product[a * channels + r : a * channels + r + rows, :]

        low = part(2)
        outer = part(0) + jnp.concatenate([low[:, 128:], low[:, 0:128]], axis=1)
        finish(r, rows, part(1)[:, 0:CELLS] + pltpu.roll(outer, SIDE, 1)[:, 0:CELLS])


def conv_kernel(
    field,
    above,
    below,
    links,
    weight1,
    weight2,
    scale,
    bias,
    out_bias,
    out,
    stack,
    product,
    side_stack,
    side_product,
    hidden,
    result,
    sems,
):
    channels = field.shape[0]

    def gate(tile, n, want):
        return jnp.where(links[tile, n] == want, 1.0, 0.0)

    def blend(sources, gates):
        return sources[0] * gates[0] + sources[1] * gates[1]

    def halo(low, high, tile):
        def pick(down, up):
            return halves(
                blend(low, [gate(tile, down, k) for k in range(2)]),
                blend(high, [gate(tile, up, k) for k in range(2)]),
            )

        return lane_images(pick(6, 1), pick(5, 0), pick(7, 2))

    def pair(ref):
        return [ref[:, k * 128 : (k + 1) * 128].astype(F32) for k in range(2)]

    upper, lower = pair(above), pair(below)

    for tile in range(2):
        stack_tile(field, links, tile, stack.at[tile])
        stack_lanes(stack.at[tile], CELLS, halo(lower, upper, tile))
        multiply(weight1, stack.at[tile], product.at[tile])

        def finish(r, rows, summed):
            active = jnp.maximum(scale[r : r + rows, :] * summed + bias[r : r + rows, :], 0.0)
            hidden[r : r + rows, tile * CELLS : (tile + 1) * CELLS] = active.astype(BF)

        sum_tile(product.at[tile], finish)

    first = [field[:, j * CELLS : j * CELLS + 128].astype(F32) for j in range(2)]
    last = [field[:, (j + 1) * CELLS - 128 : (j + 1) * CELLS].astype(F32) for j in range(2)]

    def joined(west, center, east):
        found = 0.0
        for j in range(2):
            for a, b in ((west, center), (center, east)):
                found = jnp.maximum(found, gate(j, a, 0) * gate(j, b, 1))
        return found

    joined_up, joined_down = joined(0, 1, 2), joined(5, 6, 7)
    for k in range(2):
        for start, source, flag in ((0, upper, joined_up), (256, lower, joined_down)):
            other = source[1 - k] * flag
            none = jnp.zeros_like(other)
            images = lane_images(source[k], other if k else none, none if k else other)
            stack_lanes(side_stack, start + k * 128, images)

        def own(up, down):
            return halves(
                blend(first, [gate(j, up, k) for j in range(2)]),
                blend(last, [gate(j, down, k) for j in range(2)]),
            )

        stack_lanes(side_stack, 512 + k * 128, lane_images(own(1, 6), own(2, 7), own(0, 5)))
    multiply(weight1, side_stack, side_product)
    sides = []
    for k in range(2):

        def part(a, kind):
            start = kind * 256 + k * 128
            return side_product[a * channels : (a + 1) * channels, start : start + 128]

        down_row = part(1, 1) + pltpu.roll(part(2, 1) + part(0, 2), SIDE, 1)
        up_row = part(1, 0) + pltpu.roll(part(0, 0) + part(2, 2), SIDE, 1)
        summed = halves(down_row, up_row)
        active = jnp.maximum(scale[...] * summed + bias[...], 0.0)
        sides.append(active.astype(BF).astype(F32))

    copies = []
    for tile in range(2):
        stack_tile(hidden, links, tile, stack.at[tile])
        stack_lanes(stack.at[tile], CELLS, halo(sides, sides, tile))
        multiply(weight2, stack.at[tile], product.at[tile])

        def finish(r, rows, summed):
            result[tile, r : r + rows, :] = summed + out_bias[r : r + rows, :]
            copy = pltpu.make_async_copy(
                result.at[tile, r : r + rows],
                out.at[tile, r : r + rows],
                sems.at[tile, r // rows],
            )
            copy.start()
            copies.append(copy)

        sum_tile(product.at[tile], finish)
    for copy in copies:
        copy.wait()


def convolutions(field, above, below, links, weight1, weight2, scale, bias, out_bias):
    channels = field.shape[0]
    span = CELLS + 128
    return pl.pallas_call(
        conv_kernel,
        out_shape=jax.ShapeDtypeStruct((2, channels, CELLS), F32),
        in_specs=[VMEM, VMEM, VMEM, SMEM] + [VMEM] * 5,
        out_specs=pl.BlockSpec(memory_space=pl.ANY),
        scratch_shapes=[
            pltpu.VMEM((2, 3 * channels, span), BF),
            pltpu.VMEM((2, 3 * channels, span), F32),
            pltpu.VMEM((3 * channels, 768), BF),
            pltpu.VMEM((3 * channels, 768), F32),
            pltpu.VMEM((channels, 2 * CELLS), BF),
            pltpu.VMEM((2, channels, CELLS), F32),
            pltpu.SemaphoreType.DMA((2, channels // 16)),
        ],
        compiler_params=params(40),
    )(field, above, below, links, weight1, weight2, scale, bias, out_bias)


def exchange(tops, bottoms):
    devices = lax.axis_size("dev")
    above = lax.ppermute(bottoms, "dev", [(i, i + 1) for i in range(devices - 1)])
    below = lax.ppermute(tops, "dev", [(i + 1, i) for i in range(devices - 1)])
    return above, below


def by_row_tap(weight):
    channels = weight.shape[0]
    return weight.reshape(channels, 3, 3 * channels).transpose(1, 0, 2).reshape(3 * channels, -1)


def per_device(
    context,
    depth_logits,
    send_point,
    recv_cell,
    neighbour,
    conv1_weight,
    layer_scale,
    layer_bias,
    conv2_weight,
    out_bias,
):
    lifted = lift(context, depth_logits, send_point[0])
    arrived = [
        lax.all_to_all(part, "dev", split_axis=0, concat_axis=0, tiled=True) for part in lifted
    ]
    bev, tops, bottoms = splat(arrived[0], recv_cell[0])
    above, below = exchange(tops, bottoms)
    out = convolutions(
        bev,
        above,
        below,
        neighbour[0],
        by_row_tap(conv1_weight),
        by_row_tap(conv2_weight),
        layer_scale[:, None],
        layer_bias[:, None],
        out_bias[:, None],
    )
    return out[None]


def solution(mesh):
    in_specs = (
        P(None, "dev"),
        P(None, "dev"),
        P("dev", None, None),
        P("dev", None, None),
        P("dev", None, None),
        P(),
        P(),
        P(),
        P(),
        P(),
    )
    out_specs = P("dev", None, None, None)
    return jax.shard_map(
        per_device, mesh=mesh, in_specs=in_specs, out_specs=out_specs, check_vma=False
    )
```

time: 120 us -> 96.1 us (0.80)
  Pallas kernels: 46.8 us -> 34.1 us
  waiting for transfers between devices: 13.6 us -> 6.72 us
  starting transfers between devices: 13.7 us -> 9.52 us
    pallas_call x4 -> x3, Pallas kernels: 46.8 us -> 34.1 us  [the longest x1 22.7 us: splat(): pl.pallas_call(functools.partial(splat_kernel, groups, 32), out_shape=sha...]
    ppermute x2 -> x1, waiting for transfers between devices: 13.6 us -> 6.72 us  [exchange(): below = lax.ppermute(tops, 'dev', [(i + 1, i) for i in range(devices - 1)])]
    ppermute x2 -> x1, starting transfers between devices: 4.32 us -> 2.1 us  [exchange(): below = lax.ppermute(tops, 'dev', [(i + 1, i) for i in range(devices - 1)])]
    ppermute x2 -> x1, starting transfers between devices: 9.36 us -> 7.42 us  [exchange(): lax.ppermute(bottoms, 'dev', [(i, i + 1) for i in range(devices - 1)])]
  transfers between devices with their start and end apart: 4 -> 2, of which waited for: 2 -> 1; matrix products, arithmetic and copies ran while one was open for 1% -> 1% of each run, Pallas kernels for 0% -> 0%
where the time goes in v1:
time: 96.1 us; the launch traced here: 95.7 us
  blocking collectives  41.9 us (44%)
  Pallas kernels  34.1 us (35%)
  starting transfers between devices  9.52 us (10%)
  waiting for transfers between devices  6.72 us (7%)
  local copies, waits for them, and re-layouts  3.12 us (3%)
    all_to_all x1, blocking collectives, per_device(): lax.all_to_all(part, 'dev', split_axis=0, concat_axis=0, tiled=True)  41.9 us
    pallas_call x1, Pallas kernels, splat(): pl.pallas_call(functools.partial(splat_kernel, groups, 32), out_shape=sha...  22.7 us
    pallas_call x1, Pallas kernels, convolutions(): pl.pallas_call(conv_kernel, out_shape=jax.ShapeDtypeStruct((2, channels,...  8.68 us
    ppermute x1, starting transfers between devices, exchange(): lax.ppermute(bottoms, 'dev', [(i, i + 1) for i in range(devices - 1)])  7.42 us
    ppermute x1, waiting for transfers between devices, exchange(): below = lax.ppermute(tops, 'dev', [(i + 1, i) for i in range(devices - 1)])  6.72 us
    pallas_call x1, Pallas kernels, lift(): pl.pallas_call(functools.partial(lift_kernel, 32), out_shape=[jax.ShapeDt...  2.72 us
    unnamed x20, local copies, waits for them, and re-layouts  2.48 us
    ppermute x1, starting transfers between devices, exchange(): below = lax.ppermute(tops, 'dev', [(i + 1, i) for i in range(devices - 1)])  2.1 us
  transfers between devices with their start and end apart: 2, of which 1 were waited for; matrix products, arithmetic and copies ran while one was open for 1% of the time, Pallas kernels for 0%

profile of v1, /device:TPU:31, one launch (start us, length us, event | category | flops | bytes accessed | tf_op | source)
XLA Modules:
  0.0 95.7 jit_solution(12871369719095693185)
XLA Ops:
  0.0 0.0 copy-start
  0.0 0.8 copy-done
  0.8 0.0 copy-start.1
  0.8 0.8 copy-done.1
  1.7 0.0 copy-start.2
  1.7 0.8 copy-done.2
  2.4 2.7 %shard_map.100 = bf16[128,80,128]{2,1,0:T(8,128)(2,1)S(1)} custom-call(bf16[80,256]{1,0:T(8,128)(2,1)S(1)} %copy-done.2, bf16[118,256]{1,0:T(8,128)(2,1)S(1)} %copy-done.1, s32[128,128]{1,0:T(8,128)S(1)} %bitcast.13), custom_call_target="tpu_custom_call" | custom-call | tf_op jit(solution)/shard_map/pallas_call | solution.py:87
  5.2 0.0 copy-start.4
  5.2 41.9 %all_to_all.5.arrived = bf16[128,80,128]{2,1,0:T(8,128)(2,1)S(1)} all-to-all(bf16[128,80,128]{2,1,0:T(8,128)(2,1)S(1)} %shard_map.100), channel_id=1, replica_groups=mesh['dev'=128] {'dev'}, dimensions={0} | all-to-all | bytes 5242880 | tf_op jit(solution)/shard_map/all_to_all | solution.py:387
  47.1 0.0 copy-done.4
  47.1 0.0 copy-start.5
  47.1 0.0 copy-start.6
  47.1 0.0 copy-start.8
  47.1 0.0 copy-start.9
  47.1 0.0 copy-start.3
  47.1 22.7 %shard_map.101 = (bf16[80,8192]{1,0:T(8,128)(2,1)S(1)}, bf16[80,256]{1,0:T(8,128)(2,1)S(1)}, bf16[80,256]{1,0:T(8,128)(2,1)S(1)}) custom-call(bf16[128,80,128]{2,1,0:T(8,128)(2,1)S(1)} %all_to_all.5.arrived, s32[128,128]{1,0:T(8,128)S(1)} %bitcast.15), custom_call_target="tpu_custom_call" | custom-call | flops 21474836480 | bytes 3932160 | tf_op jit(solution)/shard_map/pallas_call | solution.py:152
  69.9 7.4 %collective-permute-start = (bf16[80,256]{1,0:T(8,128)(2,1)S(1)}, bf16[80,256]{1,0:T(8,128)(2,1)S(1)}, u32[]{:S(2)}, u32[]{:S(2)}) collective-permute-start(bf16[80,256]{1,0:T(8,128)(2,1)S(1)} %get-tuple-element.9), channel_id=1, source_target_pairs={{0,1},{1,2},{2,3},{3,4},{4,5},{5,6},{6,7},{7,8},{8,9},{9,10},{10,1... | collective-permute-start | bytes 122888 | tf_op jit(solution)/shard_map/ppermute | solution.py:363
  77.3 2.1 %collective-permute-start.1 = (bf16[80,256]{1,0:T(8,128)(2,1)S(1)}, bf16[80,256]{1,0:T(8,128)(2,1)S(1)}, u32[]{:S(2)}, u32[]{:S(2)}) collective-permute-start(bf16[80,256]{1,0:T(8,128)(2,1)S(1)} %get-tuple-element.10), channel_id=1, source_target_pairs={{1,0},{2,1},{3,2},{4,3},{5,4},{6,5},{7,6},{8,7},{9,8},{10,9},{11,1... | collective-permute-start | bytes 122888 | tf_op jit(solution)/shard_map/ppermute | solution.py:364
  79.4 0.0 copy-done.5
  79.4 0.2 reshape.12
  79.6 0.0 copy-done.6
  79.6 0.2 reshape.14
  79.8 0.0 copy-done.7
  79.8 0.1 copy.18.scale
  79.9 0.0 copy-done.8
  79.9 0.1 copy.19.bias
  80.0 0.0 copy-done.9
  80.0 0.1 copy.20.out_bias
  80.1 0.0 collective-permute-done.above
  80.2 6.7 %collective-permute-done.1.below = bf16[80,256]{1,0:T(8,128)(2,1)S(1)} collective-permute-done((bf16[80,256]{1,0:T(8,128)(2,1)S(1)}, bf16[80,256]{1,0:T(8,128)(2,1)S(1)}, u32[]{:S(2)}, u32[]{:S(2)}) %collective-permute-start.1) | collective-permute-done | bytes 40992 | tf_op jit(solution)/shard_map/ppermute | solution.py:364
  86.9 0.0 copy-done.3
  86.9 8.7 %shard_map.102 = f32[2,80,4096]{2,1,0:T(8,128)} custom-call(bf16[80,8192]{1,0:T(8,128)(2,1)S(1)} %get-tuple-element.8.field, bf16[80,256]{1,0:T(8,128)(2,1)S(1)} %collective-permute-done.above, bf16[80,256]{1,0:T(8,128)(2,1)S(1)} %collective-permute-done.1.below, s32[2,8]{1,0:T(2,128)S(1)} %bitcast.14, bf16[240,240]{1,0:T(8,128)(2,1)S(1)} %bitcast.11, ...), custom_call_target="tpu_custom_call" | custom-call | tf_op jit(solution)/shard_map/pallas_call | solution.py:343
  (3 shorter events, 0.0 us)
Async XLA Ops:
  0.0 0.8 copy-start
  0.8 0.8 copy-start.1
  1.7 0.8 copy-start.2
  5.2 41.9 %copy-start.4 = (s32[1,128,128]{2,1,0:T(8,128)S(1)}, s32[1,128,128]{2,1,0:T(8,128)}, u32[]{:S(2)}) copy-start(s32[1,128,128]{2,1,0:T(8,128)} %param.13) | copy-start | bytes 196612
  47.1 32.3 %copy-start.5 = (bf16[80,720]{1,0:T(8,128)(2,1)S(1)}, bf16[80,720]{1,0:T(8,128)(2,1)}, u32[]{:S(2)}) copy-start(bf16[80,720]{1,0:T(8,128)(2,1)} %param.15) | copy-start | bytes 345604
  47.1 32.5 %copy-start.6 = (bf16[80,720]{1,0:T(8,128)(2,1)S(1)}, bf16[80,720]{1,0:T(8,128)(2,1)}, u32[]{:S(2)}) copy-start(bf16[80,720]{1,0:T(8,128)(2,1)} %param.18) | copy-start | bytes 345604
  47.1 32.7 %copy-start.7 = (f32[80]{0:T(128)S(1)}, f32[80]{0:T(128)}, u32[]{:S(2)}) copy-start(f32[80]{0:T(128)} %param.16) | copy-start | bytes 964
  47.1 32.8 %copy-start.8 = (f32[80]{0:T(128)S(1)}, f32[80]{0:T(128)}, u32[]{:S(2)}) copy-start(f32[80]{0:T(128)} %param.17) | copy-start | bytes 964
  47.1 32.9 %copy-start.9 = (f32[80]{0:T(128)S(1)}, f32[80]{0:T(128)}, u32[]{:S(2)}) copy-start(f32[80]{0:T(128)} %param.19) | copy-start | bytes 964
  47.1 39.7 %copy-start.3 = (s32[1,2,8]{2,1,0:T(2,128)S(1)}, s32[1,2,8]{2,1,0:T(2,128)}, u32[]{:S(2)}) copy-start(s32[1,2,8]{2,1,0:T(2,128)} %param.14) | copy-start | bytes 196
  69.9 10.2 %collective-permute-start = (bf16[80,256]{1,0:T(8,128)(2,1)S(1)}, bf16[80,256]{1,0:T(8,128)(2,1)S(1)}, u32[]{:S(2)}, u32[]{:S(2)}) collective-permute-start(bf16[80,256]{1,0:T(8,128)(2,1)S(1)} %get-tuple-element.9), channel_id=1, source_target_pairs={{0,1},{1,2},{2,3},{3,4},{4,5},{5,6},{6,7},{7,8},{8,9},{9,10},{10,1... | collective-permute-start | bytes 122888 | tf_op jit(solution)/shard_map/ppermute | solution.py:363
  77.3 9.5 %collective-permute-start.1 = (bf16[80,256]{1,0:T(8,128)(2,1)S(1)}, bf16[80,256]{1,0:T(8,128)(2,1)S(1)}, u32[]{:S(2)}, u32[]{:S(2)}) collective-permute-start(bf16[80,256]{1,0:T(8,128)(2,1)S(1)} %get-tuple-element.10), channel_id=1, source_target_pairs={{1,0},{2,1},{3,2},{4,3},{5,4},{6,5},{7,6},{8,7},{9,8},{10,9},{11,1... | collective-permute-start | bytes 122888 | tf_op jit(solution)/shard_map/ppermute | solution.py:364

commit v2 on v1

v2 whole, which is shorter than its diff:
```python
import functools

import jax
import jax.numpy as jnp
from jax import lax
from jax.experimental import pallas as pl
from jax.experimental.pallas import tpu as pltpu
from jax.sharding import PartitionSpec as P

SIDE = 64
CELLS = SIDE * SIDE
BF = jnp.bfloat16
F32 = jnp.float32
VMEM = pl.BlockSpec(memory_space=pltpu.VMEM)
SMEM = pl.BlockSpec(memory_space=pltpu.SMEM)


def params(megabytes):
    return pltpu.CompilerParams(vmem_limit_bytes=megabytes * 1024 * 1024)


def float_iota(shape, axis):
    return lax.broadcasted_iota(jnp.int32, shape, axis).astype(F32).astype(BF)


def split_high(value):
    high = value.astype(BF).astype(F32)
    return high, value - high


def lift_kernel(unroll, context_in, logits_in, send_in, out, lifted, context, logits, send, wide, table, sems):
    pairs = ((logits_in, logits), (context_in, context), (send_in, send))
    copies = [pltpu.make_async_copy(a, b, sems.at[n]) for n, (a, b) in enumerate(pairs)]
    for copy in copies:
        copy.start()
    channels, pixels = context.shape
    depths = logits.shape[0]
    slots = send.shape[1]
    bins = -(-depths // 8) * 8
    copies[0].wait()
    values = logits[...].astype(F32)
    largest = jnp.max(values, axis=0, keepdims=True)
    inverse = 1.0 / jnp.sum(jnp.exp(values - largest), axis=0, keepdims=True)
    wide[...] = jnp.zeros(wide.shape, F32)
    wide[0:depths, :] = values
    wide[bins : bins + 1, :] = largest
    for n in range(3):
        high, inverse = split_high(inverse)
        wide[bins + 1 + n : bins + 2 + n, :] = high
    copies[1].wait()
    copies[2].wait()
    table[0:channels, :] = context[...]
    table[channels:, :] = wide[...].astype(BF)
    pixel_iota = float_iota((pixels, slots), 0)
    bin_iota = lax.broadcasted_iota(jnp.int32, (8, slots), 0)
    one, zero = jnp.ones((), BF), jnp.zeros((), BF)

    def step(i, carry):
        points = [send[pl.ds(i * unroll + u, 1), :] for u in range(unroll)]
        picks = []
        for point in points:
            pixel = (point & (pixels - 1)).astype(F32).astype(BF)
            picks.append(jnp.where(pixel_iota == pixel, one, zero))
        for v in range(0, unroll, 2):
            found = jnp.dot(
                table[...], jnp.concatenate(picks[v : v + 2], axis=1), preferred_element_type=F32
            )
            for u in (v, v + 1):
                point = points[u]
                mine = found[:, (u - v) * slots : (u - v + 1) * slots]
                offset = (point >> 8) - bin_iota
                chosen = jnp.zeros((8, slots), F32)
                for r in range(0, bins, 8):
                    chosen = jnp.where(offset == r, mine[channels + r : channels + r + 8], chosen)
                logit = jnp.sum(chosen, axis=0, keepdims=True)
                tail = mine[channels + bins :]
                scale = tail[1:2] + tail[2:3] + tail[3:4]
                weight = jnp.exp(logit - tail[0:1]) * scale
                weight = jnp.where(point >= 0, weight, 0.0)
                lifted[i * unroll + u] = (mine[0:channels] * weight).astype(BF)
        leave(i).start()
        return carry

    def leave(i):
        at = pl.ds(i * unroll, unroll)
        return pltpu.make_async_copy(lifted.at[at], out.at[at], sems.at[3 + i])

    lax.fori_loop(0, send.shape[0] // unroll, step, 0)
    for i in range(send.shape[0] // unroll):
        leave(i).wait()


def lift(context, logits, send):
    channels, pixels = context.shape
    return pl.pallas_call(
        functools.partial(lift_kernel, 32),
        out_shape=jax.ShapeDtypeStruct((send.shape[0], channels, send.shape[1]), BF),
        in_specs=[pl.BlockSpec(memory_space=pl.ANY)] * 3,
        out_specs=pl.BlockSpec(memory_space=pl.ANY),
        scratch_shapes=[
            pltpu.VMEM((send.shape[0], channels, send.shape[1]), BF),
            pltpu.VMEM(context.shape, BF),
            pltpu.VMEM(logits.shape, BF),
            pltpu.VMEM(send.shape, jnp.int32),
            pltpu.VMEM((128, pixels), F32),
            pltpu.VMEM((channels + 128, pixels), BF),
            pltpu.SemaphoreType.DMA((3 + send.shape[0] // 32,)),
        ],
        compiler_params=params(60),
    )(context, logits, send)


def field_edges(field, tops, bottoms):
    tops[...] = field[:, 0:256]
    bottoms[...] = field[:, 2 * CELLS - 256 : 2 * CELLS]


def splat_kernel(groups, unroll, arrived, cells, *rest):
    *before, bev = rest[: len(rest) - 1 if len(rest) == 2 else len(rest) - 3]
    total = rest[-1]
    channels, slots = arrived.shape[1:]
    width = total.shape[1]
    shift = width.bit_length() - 1
    block = 256
    total[...] = jnp.zeros(total.shape, F32)
    cell_iota = float_iota((block, slots * unroll), 0)
    one, zero = jnp.ones((), BF), jnp.zeros((), BF)

    def step(i, carry):
        values = jnp.concatenate([arrived[i * unroll + u] for u in range(unroll)], axis=1)
        targets = jnp.concatenate([cells[pl.ds(i * unroll + u, 1), :] for u in range(unroll)], axis=1)
        row, x = (targets >> 6) & (SIDE - 1), targets & (SIDE - 1)
        targets = jnp.where(targets < 0, -1, row * 128 + (targets >> 12) * SIDE + x)
        group = targets >> shift
        place = targets & (width - 1)
        masked = []
        for g in range(groups):
            masked.append(values * jnp.where(group == g, 1.0, 0.0).astype(BF))
        grouped = jnp.concatenate(masked, axis=0)
        for j in range(width // block):
            spot = (place - j * block).astype(F32).astype(BF)
            pick = jnp.where(cell_iota == spot, one, zero)
            total[:, j * block : (j + 1) * block] += lax.dot_general(
                grouped, pick, (((1,), (1,)), ((), ())), preferred_element_type=F32
            )
        return carry

    lax.fori_loop(0, arrived.shape[0] // unroll, step, 0)
    first = bev.shape[0] - channels
    if before:
        bev[0:first, :] = before[0][...]
    for g in range(groups):
        bev[first:, g * width : (g + 1) * width] = total[g * channels : (g + 1) * channels, :].astype(BF)
    if len(rest) > 2:
        field_edges(bev, rest[-3], rest[-2])


def splat(arrived, cells, before=None, last=True):
    channels = arrived.shape[1]
    groups = 4
    while groups * channels < 256:
        groups *= 2
    width = 2 * CELLS // groups
    total = channels + (0 if before is None else before.shape[0])
    edge = jax.ShapeDtypeStruct((total, 256), BF)
    shapes = (jax.ShapeDtypeStruct((total, 2 * CELLS), BF),) + ((edge, edge) if last else ())
    operands = (arrived, cells) + (() if before is None else (before,))
    return pl.pallas_call(
        functools.partial(splat_kernel, groups, 32),
        out_shape=shapes,
        in_specs=[VMEM] * len(operands),
        out_specs=(VMEM,) * len(shapes),
        scratch_shapes=[pltpu.VMEM((groups * channels, width), F32)],
        compiler_params=params(32),
        cost_estimate=pl.CostEstimate(
            flops=2 * arrived.shape[0] * 128 * 2 * CELLS * channels,
            bytes_accessed=arrived.size * 2 + total * 2 * CELLS * 2,
            transcendentals=0,
        ),
    )(*operands)


def conv_kernel(
    field,
    above,
    below,
    links,
    weight1,
    weight2,
    scale,
    bias,
    out_bias,
    out,
    stack1,
    stack2,
    side_stack,
    result,
    sems,
):
    channels = field.shape[0]
    shape = (channels, 128)
    lane = lax.broadcasted_iota(jnp.int32, shape, 1)
    lower = lane < SIDE
    column = lane & (SIDE - 1)

    def gate(tile, n, want):
        return jnp.where(links[tile, n] == want, 1.0, 0.0)

    def block(ref, y):
        return ref[:, y * 128 : (y + 1) * 128]

    def put(stack, slot, left, center, right):
        for b, image in enumerate((left, center, right)):
            stack[b * channels : (b + 1) * channels, slot * 128 : (slot + 1) * 128] = image.astype(BF)

    def keeps(joined):
        left = jnp.where(lane == 0, 0.0, jnp.where(lane == SIDE, joined, 1.0))
        right = jnp.where(lane == 127, 0.0, jnp.where(lane == SIDE - 1, joined, 1.0))
        return left, right

    def put_row(stack, slot, row, keep):
        wide = row.astype(F32)
        put(stack, slot, pltpu.roll(wide, 1, 1) * keep[0], row, pltpu.roll(wide, 127, 1) * keep[1])

    def put_mapped(stack, slot, source, west, center, east, inverse=False):
        swapped = pltpu.roll(source, SIDE, 1)

        def mapped(n):
            cross = [gate(0, n, 1), gate(1, n, 0)]
            if inverse:
                cross.reverse()
            same = jnp.where(lower, gate(0, n, 0), gate(1, n, 1))
            return source * same + swapped * jnp.where(lower, cross[0], cross[1])

        middle = mapped(center)
        left = jnp.where(column == 0, pltpu.roll(mapped(west), SIDE + 1, 1), pltpu.roll(middle, 1, 1))
        right = jnp.where(
            column == SIDE - 1, pltpu.roll(mapped(east), SIDE - 1, 1), pltpu.roll(middle, 127, 1)
        )
        put(stack, slot, left, middle, right)

    def multiply(weight, stack, product, start, stop):
        found = jnp.dot(
            weight[...], stack[:, start * 128 : stop * 128], preferred_element_type=F32
        )
        for slot in range(start, stop):
            lanes = slice((slot - start) * 128, (slot - start + 1) * 128)
            for a in range(3):
                product[a, slot] = found[a * channels : (a + 1) * channels, lanes]

    def summed(product, slots):
        first, second, third = (product.pop((a, slot)) for a, slot in enumerate(slots))
        return first + second + third

    def joined(west, center, east):
        found = 0.0
        for j in range(2):
            for a, b in ((west, center), (center, east)):
                found = jnp.maximum(found, gate(j, a, 0) * gate(j, b, 1))
        return found

    gain = jnp.broadcast_to(scale[...], shape)
    shift = jnp.broadcast_to(bias[...], shape)
    last_shift = jnp.broadcast_to(out_bias[...], shape)
    keep = keeps(gate(1, 3, 0))
    keep_up, keep_down = keeps(joined(0, 1, 2)), keeps(joined(5, 6, 7))
    end = SIDE + 1
    product1, product2, side_product = {}, {}, {}

    def activate(value):
        return jnp.maximum(gain * value + shift, 0.0).astype(BF)

    put_row(side_stack, 0, block(above, 0), keep_up)
    put_row(side_stack, 1, block(above, 1), keep_up)
    put_mapped(side_stack, 2, block(field, 0).astype(F32), 2, 1, 0, True)
    put_mapped(side_stack, 3, block(field, SIDE - 1).astype(F32), 7, 6, 5, True)
    put_row(side_stack, 4, block(below, 0), keep_down)
    put_row(side_stack, 5, block(below, 1), keep_down)
    multiply(weight1, side_stack, side_product, 0, 6)
    up_row = activate(summed(side_product, (0, 1, 2))).astype(F32)
    down_row = activate(summed(side_product, (3, 4, 5))).astype(F32)
    put_mapped(stack2, 0, up_row, 0, 1, 2)
    put_mapped(stack2, end, down_row, 5, 6, 7)
    put_mapped(stack1, 0, block(above, 1).astype(F32), 0, 1, 2)
    put_mapped(stack1, end, block(below, 0).astype(F32), 5, 6, 7)

    step = 16
    done = 0
    for start in range(0, SIDE + 2, step):
        stop = min(start + step, SIDE + 2)
        for slot in range(max(start, 1), min(stop, end)):
            put_row(stack1, slot, block(field, slot - 1), keep)
        multiply(weight1, stack1, product1, start, stop)
        while done < stop - 2:
            put_row(stack2, done + 1, activate(summed(product1, (done, done + 1, done + 2))), keep)
            done += 1

    copies = []
    done = 0
    part = 16
    for start in range(0, SIDE + 2, step):
        stop = min(start + step, SIDE + 2)
        multiply(weight2, stack2, product2, start, stop)
        while done + 1 < stop - 2:
            even = summed(product2, (done, done + 1, done + 2)) + last_shift
            odd = summed(product2, (done + 1, done + 2, done + 3)) + last_shift
            at = slice(done * SIDE, (done + 2) * SIDE)
            result[0, :, at] = jnp.where(lower, even, pltpu.roll(odd, SIDE, 1))
            result[1, :, at] = jnp.where(lower, pltpu.roll(even, SIDE, 1), odd)
            done += 2
            if done % part == 0:
                n = done // part - 1
                at = slice(n * part * SIDE, (n + 1) * part * SIDE)
                for tile in range(2):
                    copy = pltpu.make_async_copy(
                        result.at[tile, :, at], out.at[tile, :, at], sems.at[tile, n]
                    )
                    copy.start()
                    copies.append(copy)
    for copy in copies:
        copy.wait()


def convolutions(field, above, below, links, weight1, weight2, scale, bias, out_bias):
    channels = field.shape[0]
    stack = pltpu.VMEM((3 * channels, (SIDE + 2) * 128), BF)
    return pl.pallas_call(
        conv_kernel,
        out_shape=jax.ShapeDtypeStruct((2, channels, CELLS), F32),
        in_specs=[VMEM, VMEM, VMEM, SMEM] + [VMEM] * 5,
        out_specs=pl.BlockSpec(memory_space=pl.ANY),
        scratch_shapes=[
            stack,
            stack,
            pltpu.VMEM((3 * channels, 768), BF),
            pltpu.VMEM((2, channels, CELLS), F32),
            pltpu.SemaphoreType.DMA((2, 4)),
        ],
        compiler_params=params(44),
    )(field, above, below, links, weight1, weight2, scale, bias, out_bias)


def exchange(tops, bottoms):
    devices = lax.axis_size("dev")
    above = lax.ppermute(bottoms, "dev", [(i, i + 1) for i in range(devices - 1)])
    below = lax.ppermute(tops, "dev", [(i + 1, i) for i in range(devices - 1)])
    return above, below


def by_row_tap(weight):
    channels = weight.shape[0]
    return weight.reshape(channels, 3, 3 * channels).transpose(1, 0, 2).reshape(3 * channels, -1)


def per_device(
    context,
    depth_logits,
    send_point,
    recv_cell,
    neighbour,
    conv1_weight,
    layer_scale,
    layer_bias,
    conv2_weight,
    out_bias,
):
    lifted = lift(context, depth_logits, send_point[0])
    arrived = lax.all_to_all(lifted, "dev", split_axis=0, concat_axis=0, tiled=True)
    bev, tops, bottoms = splat(arrived, recv_cell[0])
    above, below = exchange(tops, bottoms)
    out = convolutions(
        bev,
        above,
        below,
        neighbour[0],
        by_row_tap(conv1_weight),
        by_row_tap(conv2_weight),
        layer_scale[:, None],
        layer_bias[:, None],
        out_bias[:, None],
    )
    return out[None]


def solution(mesh):
    in_specs = (
        P(None, "dev"),
        P(None, "dev"),
        P("dev", None, None),
        P("dev", None, None),
        P("dev", None, None),
        P(),
        P(),
        P(),
        P(),
        P(),
    )
    out_specs = P("dev", None, None, None)
    return jax.shard_map(
        per_device, mesh=mesh, in_specs=in_specs, out_specs=out_specs, check_vma=False
    )
```

time: 96.1 us -> 92.2 us (0.959)
  local copies, waits for them, and re-layouts: 3.12 us -> 0.68 us
  Pallas kernels: 34.1 us -> 32.7 us
    pallas_call x1, Pallas kernels: 8.68 us -> 5.55 us  [convolutions(): pl.pallas_call(conv_kernel, out_shape=jax.ShapeDtypeStruct((2, channels,...]
    unnamed x20 -> x14, local copies, waits for them, and re-layouts: 2.48 us -> 0.04 us
    pallas_call x1, Pallas kernels: 2.72 us -> 4.44 us  [lift(): pl.pallas_call(functools.partial(lift_kernel, 32), out_shape=jax.ShapeDty...]
where the time goes in v2:
time: 92.2 us; the launch traced here: 91.9 us
  blocking collectives  42.1 us (46%)
  Pallas kernels  32.7 us (35%)
  starting transfers between devices  9.34 us (10%)
  waiting for transfers between devices  6.9 us (7%)
    all_to_all x1, blocking collectives, per_device(): lax.all_to_all(lifted, 'dev', split_axis=0, concat_axis=0, tiled=True)  42.1 us
    pallas_call x1, Pallas kernels, splat(): pl.pallas_call(functools.partial(splat_kernel, groups, 32), out_shape=sha...  22.7 us
    ppermute x1, starting transfers between devices, exchange(): lax.ppermute(bottoms, 'dev', [(i, i + 1) for i in range(devices - 1)])  7.42 us
    ppermute x1, waiting for transfers between devices, exchange(): below = lax.ppermute(tops, 'dev', [(i + 1, i) for i in range(devices - 1)])  6.9 us
    pallas_call x1, Pallas kernels, convolutions(): pl.pallas_call(conv_kernel, out_shape=jax.ShapeDtypeStruct((2, channels,...  5.55 us
    pallas_call x1, Pallas kernels, lift(): pl.pallas_call(functools.partial(lift_kernel, 32), out_shape=jax.ShapeDty...  4.44 us
    ppermute x1, starting transfers between devices, exchange(): below = lax.ppermute(tops, 'dev', [(i + 1, i) for i in range(devices - 1)])  1.92 us
  transfers between devices with their start and end apart: 2, of which 1 were waited for; matrix products, arithmetic and copies ran while one was open for 1% of the time, Pallas kernels for 0%

profile of v2, /device:TPU:31, one launch (start us, length us, event | category | flops | bytes accessed | tf_op | source)
XLA Modules:
  0.0 91.9 jit_solution(8502020407251429339)
XLA Ops:
  0.0 4.4 %shard_map.100 = bf16[128,80,128]{2,1,0:T(8,128)(2,1)} custom-call(bf16[80,256]{1,0:T(8,128)(2,1)} %context_in.1, bf16[118,256]{1,0:T(8,128)(2,1)} %logits_in.1, s32[128,128]{1,0:T(8,128)} %bitcast.17), custom_call_target="tpu_custom_call" | custom-call | tf_op jit(solution)/shard_map/pallas_call | solution.py:95
  4.4 0.0 copy-start.1
  4.5 42.1 %all_to_all.5.arrived = bf16[128,80,128]{2,1,0:T(8,128)(2,1)S(1)} all-to-all(bf16[128,80,128]{2,1,0:T(8,128)(2,1)} %shard_map.100), channel_id=1, replica_groups=mesh['dev'=128] {'dev'}, dimensions={0} | all-to-all | bytes 5242880 | tf_op jit(solution)/shard_map/all_to_all | solution.py:368
  46.6 0.0 copy-done.1
  46.6 0.0 copy-start.2
  46.6 0.0 copy-start.3
  46.6 0.0 copy-start.4
  46.6 0.0 copy-start.5
  46.6 0.0 copy-start.6
  46.6 0.0 copy-start
  46.6 22.7 %shard_map.101 = (bf16[80,8192]{1,0:T(8,128)(2,1)S(1)}, bf16[80,256]{1,0:T(8,128)(2,1)S(1)}, bf16[80,256]{1,0:T(8,128)(2,1)S(1)}) custom-call(bf16[128,80,128]{2,1,0:T(8,128)(2,1)S(1)} %all_to_all.5.arrived, s32[128,128]{1,0:T(8,128)S(1)} %bitcast.14), custom_call_target="tpu_custom_call" | custom-call | flops 21474836480 | bytes 3932160 | tf_op jit(solution)/shard_map/pallas_call | solution.py:168
  69.4 7.4 %collective-permute-start = (bf16[80,256]{1,0:T(8,128)(2,1)S(1)}, bf16[80,256]{1,0:T(8,128)(2,1)S(1)}, u32[]{:S(2)}, u32[]{:S(2)}) collective-permute-start(bf16[80,256]{1,0:T(8,128)(2,1)S(1)} %get-tuple-element.9), channel_id=1, source_target_pairs={{0,1},{1,2},{2,3},{3,4},{4,5},{5,6},{6,7},{7,8},{8,9},{9,10},{10,1... | collective-permute-start | bytes 122888 | tf_op jit(solution)/shard_map/ppermute | solution.py:345
  76.8 1.9 %collective-permute-start.1 = (bf16[80,256]{1,0:T(8,128)(2,1)S(1)}, bf16[80,256]{1,0:T(8,128)(2,1)S(1)}, u32[]{:S(2)}, u32[]{:S(2)}) collective-permute-start(bf16[80,256]{1,0:T(8,128)(2,1)S(1)} %get-tuple-element.10), channel_id=1, source_target_pairs={{1,0},{2,1},{3,2},{4,3},{5,4},{6,5},{7,6},{8,7},{9,8},{10,9},{11,1... | collective-permute-start | bytes 122888 | tf_op jit(solution)/shard_map/ppermute | solution.py:346
  78.7 0.0 copy-done.2
  78.8 0.2 reshape.12
  78.9 0.0 copy-done.3
  79.0 0.2 reshape.14
  79.1 0.0 copy-done.4
  79.1 0.1 copy.18.scale
  79.2 0.0 copy-done.5
  79.3 0.1 copy.19.bias
  79.4 0.0 copy-done.6
  79.4 0.1 copy.20.out_bias
  79.5 0.0 collective-permute-done.above
  79.5 6.9 %collective-permute-done.1.below = bf16[80,256]{1,0:T(8,128)(2,1)S(1)} collective-permute-done((bf16[80,256]{1,0:T(8,128)(2,1)S(1)}, bf16[80,256]{1,0:T(8,128)(2,1)S(1)}, u32[]{:S(2)}, u32[]{:S(2)}) %collective-permute-start.1) | collective-permute-done | bytes 40992 | tf_op jit(solution)/shard_map/ppermute | solution.py:346
  86.4 0.0 copy-done
  86.4 5.6 %shard_map.102 = f32[2,80,4096]{2,1,0:T(8,128)} custom-call(bf16[80,8192]{1,0:T(8,128)(2,1)S(1)} %get-tuple-element.8.field, bf16[80,256]{1,0:T(8,128)(2,1)S(1)} %collective-permute-done.above, bf16[80,256]{1,0:T(8,128)(2,1)S(1)} %collective-permute-done.1.below, s32[2,8]{1,0:T(2,128)S(1)} %bitcast.13, bf16[240,240]{1,0:T(8,128)(2,1)S(1)} %bitcast.11, ...), custom_call_target="tpu_custom_call" | custom-call | tf_op jit(solution)/shard_map/pallas_call | solution.py:327
  (2 shorter events, 0.0 us)
Async XLA Ops:
  4.4 42.1 %copy-start.1 = (s32[1,128,128]{2,1,0:T(8,128)S(1)}, s32[1,128,128]{2,1,0:T(8,128)}, u32[]{:S(2)}) copy-start(s32[1,128,128]{2,1,0:T(8,128)} %param.13) | copy-start | bytes 196612
  46.6 32.2 %copy-start.2 = (bf16[80,720]{1,0:T(8,128)(2,1)S(1)}, bf16[80,720]{1,0:T(8,128)(2,1)}, u32[]{:S(2)}) copy-start(bf16[80,720]{1,0:T(8,128)(2,1)} %param.15) | copy-start | bytes 345604
  46.6 32.3 %copy-start.3 = (bf16[80,720]{1,0:T(8,128)(2,1)S(1)}, bf16[80,720]{1,0:T(8,128)(2,1)}, u32[]{:S(2)}) copy-start(bf16[80,720]{1,0:T(8,128)(2,1)} %param.18) | copy-start | bytes 345604
  46.6 32.5 %copy-start.4 = (f32[80]{0:T(128)S(1)}, f32[80]{0:T(128)}, u32[]{:S(2)}) copy-start(f32[80]{0:T(128)} %param.16) | copy-start | bytes 964
  46.6 32.6 %copy-start.5 = (f32[80]{0:T(128)S(1)}, f32[80]{0:T(128)}, u32[]{:S(2)}) copy-start(f32[80]{0:T(128)} %param.17) | copy-start | bytes 964
  46.6 32.7 %copy-start.6 = (f32[80]{0:T(128)S(1)}, f32[80]{0:T(128)}, u32[]{:S(2)}) copy-start(f32[80]{0:T(128)} %param.19) | copy-start | bytes 964
  46.6 39.7 %copy-start = (s32[1,2,8]{2,1,0:T(2,128)S(1)}, s32[1,2,8]{2,1,0:T(2,128)}, u32[]{:S(2)}) copy-start(s32[1,2,8]{2,1,0:T(2,128)} %param.14) | copy-start | bytes 196
  69.4 10.1 %collective-permute-start = (bf16[80,256]{1,0:T(8,128)(2,1)S(1)}, bf16[80,256]{1,0:T(8,128)(2,1)S(1)}, u32[]{:S(2)}, u32[]{:S(2)}) collective-permute-start(bf16[80,256]{1,0:T(8,128)(2,1)S(1)} %get-tuple-element.9), channel_id=1, source_target_pairs={{0,1},{1,2},{2,3},{3,4},{4,5},{5,6},{6,7},{7,8},{8,9},{9,10},{10,1... | collective-permute-start | bytes 122888 | tf_op jit(solution)/shard_map/ppermute | solution.py:345
  76.8 9.5 %collective-permute-start.1 = (bf16[80,256]{1,0:T(8,128)(2,1)S(1)}, bf16[80,256]{1,0:T(8,128)(2,1)S(1)}, u32[]{:S(2)}, u32[]{:S(2)}) collective-permute-start(bf16[80,256]{1,0:T(8,128)(2,1)S(1)} %get-tuple-element.10), channel_id=1, source_target_pairs={{1,0},{2,1},{3,2},{4,3},{5,4},{6,5},{7,6},{8,7},{9,8},{10,9},{11,1... | collective-permute-start | bytes 122888 | tf_op jit(solution)/shard_map/ppermute | solution.py:346

commit v3 on v2

--- a/solution.py
+++ b/solution.py
@@ -115,69 +115,178 @@
     bottoms[...] = field[:, 2 * CELLS - 256 : 2 * CELLS]
 
 
-def splat_kernel(groups, unroll, arrived, cells, *rest):
-    *before, bev = rest[: len(rest) - 1 if len(rest) == 2 else len(rest) - 3]
-    total = rest[-1]
-    channels, slots = arrived.shape[1:]
-    width = total.shape[1]
+def field_place(cell):
+    row, x = (cell >> 6) & (SIDE - 1), cell & (SIDE - 1)
+    return jnp.where(cell < 0, -1, row * 128 + (cell >> 12) * SIDE + x)
+
+
+def list_starts(cells):
+    half = (cells >> 11) & 1
+    counts = jnp.stack([jnp.sum((cells >= 0) & (half == n), axis=1, dtype=jnp.int32) for n in range(2)])
+    return jnp.pad(jnp.cumsum(counts, axis=1), ((0, 0), (1, 0)))
+
+
+def start_of(starts, n, s):
+    first, last = starts[n, s], starts[n, s + 1]
+    return first >> 7, first & 127, (last >> 7) > (first >> 7)
+
+
+def plan_kernel(unroll, cells, starts, index, places, ranks, current):
+    sources, slots = cells.shape
+    below = lax.broadcasted_iota(jnp.int32, (slots, slots), 0)
+    after = lax.broadcasted_iota(jnp.int32, (slots, slots), 1)
+    earlier = jnp.where(below < after, 1.0, 0.0).astype(BF)
+    cell = cells[...]
+    for n in range(2):
+        member = jnp.where((cell >= 0) & (((cell >> 11) & 1) == n), 1.0, 0.0).astype(BF)
+        found = jnp.dot(member, earlier, preferred_element_type=F32)
+        ranks[n] = jnp.where(member.astype(F32) > 0.5, found, -1.0).astype(jnp.int32)
+        places[n] = jnp.full(places.shape[1:], -1, jnp.int32)
+    current[...] = jnp.full(current.shape, -1, jnp.int32)
+    slot_iota = float_iota((slots, slots), 0)
+    which = lax.broadcasted_iota(jnp.int32, (16, slots), 0)
+    lane = lax.broadcasted_iota(jnp.int32, (1, slots), 1)
+    one, zero = jnp.ones((), BF), jnp.zeros((), BF)
+
+    def step(i, carry):
+        for u in range(unroll):
+            s = i * unroll + u
+            place = field_place(cells[pl.ds(s, 1), :]) + 1
+            rows = jnp.where(which == 0, lane, jnp.where(which == 1, place >> 6, place & 63))
+            picks = []
+            for n in range(2):
+                rank = ranks[n, pl.ds(s, 1), :]
+                _, offset, _ = start_of(starts, n, s)
+                to = jnp.where(rank < 0, -1, (rank + offset) & 127).astype(F32).astype(BF)
+                picks.append(jnp.where(slot_iota == to, one, zero))
+            found = lax.dot_general(
+                rows.astype(F32).astype(BF),
+                jnp.concatenate(picks, axis=0),
+                (((1,), (1,)), ((), ())),
+                preferred_element_type=F32,
+            ).astype(jnp.int32)
+            for n in range(2):
+                mine = found[:, n * slots : (n + 1) * slots]
+                block, offset, full = start_of(starts, n, s)
+                index[n, pl.ds(s, 1), :] = mine[0:1]
+                place = mine[1:2] * 64 + mine[2:3] - 1
+                stored = jnp.where(lane >= offset, place, current[n : n + 1, :])
+                places[n, pl.ds(block, 1), :] = stored
+                current[n : n + 1, :] = jnp.where(full, place, stored)
+        return carry
+
+    lax.fori_loop(0, sources // unroll, step, 0)
+    for n in range(2):
+        total = starts[n, sources]
+        places[n, pl.ds(total >> 7, 1), :] = jnp.where(lane < (total & 127), current[n : n + 1, :], -1)
+
+
+LIST_BLOCK = 22
+
+
+def plan(cells, starts):
+    sources, slots = cells.shape
+    blocks = sources + 2 * LIST_BLOCK
+    return pl.pallas_call(
+        functools.partial(plan_kernel, 16),
+        out_shape=(
+            jax.ShapeDtypeStruct((2, sources, slots), jnp.int32),
+            jax.ShapeDtypeStruct((2, blocks, slots), jnp.int32),
+        ),
+        in_specs=[VMEM, SMEM],
+        out_specs=(VMEM, VMEM),
+        scratch_shapes=[pltpu.VMEM((2, sources, slots), jnp.int32), pltpu.VMEM((8, slots), jnp.int32)],
+        compiler_params=params(16),
+        cost_estimate=pl.CostEstimate(flops=10**9, bytes_accessed=10**6, transcendentals=0),
+    )(cells, starts)
+
+
+def splat_kernel(
+    groups, unroll, arrived, index, places, starts, out, tops, bottoms, lists, total, bev, sems
+):
+    sources, channels, slots = arrived.shape
+    width = total.shape[2]
     shift = width.bit_length() - 1
+    lane = lax.broadcasted_iota(jnp.int32, (channels, slots), 1)
+    nothing = jnp.zeros((channels, slots), F32)
+
+    def put(n, block, value):
+        lists[n, :, pl.ds(pl.multiple_of(block * slots, slots), slots)] = value.astype(BF)
+
+    def gather(i, carry):
+        carry = list(carry)
+        for u in range(unroll):
+            s = i * unroll + u
+            values = arrived[s].astype(F32)
+            for n in range(2):
+                block, offset, full = start_of(starts, n, s)
+                source = jnp.broadcast_to(index[n, pl.ds(s, 1), :], values.shape)
+                moved = jnp.take_along_axis(values, source, axis=1, mode="promise_in_bounds")
+                stored = jnp.where(lane >= offset, moved, carry[n])
+                put(n, block, stored)
+                carry[n] = jnp.where(full, moved, stored)
+        return tuple(carry)
+
+    rest = lax.fori_loop(0, sources // unroll, gather, (nothing, nothing))
+    for n in range(2):
+        end = starts[n, sources] >> 7
+        put(n, end, rest[n])
+        for b in range(1, LIST_BLOCK + 1):
+            put(n, end + b, nothing)
+    total[...] = jnp.zeros(total.shape, F32)
+    span = slots * LIST_BLOCK
     block = 256
-    total[...] = jnp.zeros(total.shape, F32)
-    cell_iota = float_iota((block, slots * unroll), 0)
+    cell_iota = float_iota((block, span), 0)
     one, zero = jnp.ones((), BF), jnp.zeros((), BF)
-
-    def step(i, carry):
-        values = jnp.concatenate([arrived[i * unroll + u] for u in range(unroll)], axis=1)
-        targets = jnp.concatenate([cells[pl.ds(i * unroll + u, 1), :] for u in range(unroll)], axis=1)
-        row, x = (targets >> 6) & (SIDE - 1), targets & (SIDE - 1)
-        targets = jnp.where(targets < 0, -1, row * 128 + (targets >> 12) * SIDE + x)
-        group = targets >> shift
-        place = targets & (width - 1)
-        masked = []
+    copies = []
+    for n in range(2):
+
+        def step(i, carry):
+            values = lists[n, :, pl.ds(pl.multiple_of(i * span, span), span)]
+            rows = [places[n, pl.ds(i * LIST_BLOCK + u, 1), :] for u in range(LIST_BLOCK)]
+            target = jnp.concatenate(rows, axis=1)
+            target = jnp.where(target < 0, -1, target - n * CELLS)
+            group = target >> shift
+            place = target & (width - 1)
+            masked = [values * jnp.where(group == g, 1.0, 0.0).astype(BF) for g in range(groups)]
+            grouped = jnp.concatenate(masked, axis=0)
+            for j in range(width // block):
+                spot = (place - j * block).astype(F32).astype(BF)
+                pick = jnp.where(cell_iota == spot, one, zero)
+                total[n, :, j * block : (j + 1) * block] += lax.dot_general(
+                    grouped, pick, (((1,), (1,)), ((), ())), preferred_element_type=F32
+                )
+            return carry
+
+        lax.fori_loop(0, (starts[n, sources] + span - 1) // span, step, 0)
         for g in range(groups):
-            masked.append(values * jnp.where(group == g, 1.0, 0.0).astype(BF))
-        grouped = jnp.concatenate(masked, axis=0)
-        for j in range(width // block):
-            spot = (place - j * block).astype(F32).astype(BF)
-            pick = jnp.where(cell_iota == spot, one, zero)
-            total[:, j * block : (j + 1) * block] += lax.dot_general(
-                grouped, pick, (((1,), (1,)), ((), ())), preferred_element_type=F32
-            )
-        return carry
-
-    lax.fori_loop(0, arrived.shape[0] // unroll, step, 0)
-    first = bev.shape[0] - channels
-    if before:
-        bev[0:first, :] = before[0][...]
-    for g in range(groups):
-        bev[first:, g * width : (g + 1) * width] = total[g * channels : (g + 1) * channels, :].astype(BF)
-    if len(rest) > 2:
-        field_edges(bev, rest[-3], rest[-2])
-
-
-def splat(arrived, cells, before=None, last=True):
-    channels = arrived.shape[1]
+            at = slice(n * CELLS + g * width, n * CELLS + (g + 1) * width)
+            bev[:, at] = total[n, g * channels : (g + 1) * channels, :].astype(BF)
+        at = slice(n * CELLS, (n + 1) * CELLS)
+        copies.append(pltpu.make_async_copy(bev.at[:, at], out.at[:, at], sems.at[n]))
+        copies[n].start()
+    field_edges(bev, tops, bottoms)
+    for copy in copies:
+        copy.wait()
+
+
+def splat(arrived, index, places, starts):
+    sources, channels, slots = arrived.shape
     groups = 4
-    while groups * channels < 256:
-        groups *= 2
-    width = 2 * CELLS // groups
-    total = channels + (0 if before is None else before.shape[0])
-    edge = jax.ShapeDtypeStruct((total, 256), BF)
-    shapes = (jax.ShapeDtypeStruct((total, 2 * CELLS), BF),) + ((edge, edge) if last else ())
-    operands = (arrived, cells) + (() if before is None else (before,))
+    edge = jax.ShapeDtypeStruct((channels, 256), BF)
     return pl.pallas_call(
-        functools.partial(splat_kernel, groups, 32),
-        out_shape=shapes,
-        in_specs=[VMEM] * len(operands),
-        out_specs=(VMEM,) * len(shapes),
-        scratch_shapes=[pltpu.VMEM((groups * channels, width), F32)],
+        functools.partial(splat_kernel, groups, 16),
+        out_shape=(jax.ShapeDtypeStruct((channels, 2 * CELLS), BF), edge, edge),
+        in_specs=[VMEM, VMEM, VMEM, SMEM],
+        out_specs=(pl.BlockSpec(memory_space=pl.ANY), VMEM, VMEM),
+        scratch_shapes=[
+            pltpu.VMEM((2, channels, (sources + 2 * LIST_BLOCK) * slots), BF),
+            pltpu.VMEM((2, groups * channels, CELLS // groups), F32),
+            pltpu.VMEM((channels, 2 * CELLS), BF),
+            pltpu.SemaphoreType.DMA((2,)),
+        ],
         compiler_params=params(32),
-        cost_estimate=pl.CostEstimate(
-            flops=2 * arrived.shape[0] * 128 * 2 * CELLS * channels,
-            bytes_accessed=arrived.size * 2 + total * 2 * CELLS * 2,
-            transcendentals=0,
-        ),
-    )(*operands)
+    )(arrived, index, places, starts)
 
 
 def conv_kernel(
@@ -366,7 +475,9 @@
 ):
     lifted = lift(context, depth_logits, send_point[0])
     arrived = lax.all_to_all(lifted, "dev", split_axis=0, concat_axis=0, tiled=True)
-    bev, tops, bottoms = splat(arrived, recv_cell[0])
+    starts = list_starts(recv_cell[0])
+    index, places = plan(recv_cell[0], starts)
+    bev, tops, bottoms = splat(arrived, index, places, starts)
     above, below = exchange(tops, bottoms)
     out = convolutions(
         bev,

time: 92.2 us -> 88.2 us (0.957)
  blocking collectives: 42.1 us -> 0 us
  waiting for transfers between devices: 6.9 us -> 33.8 us
  starting transfers between devices: 9.34 us -> 19.9 us
  local copies, waits for them, and re-layouts: 0.68 us -> 3.12 us
  Pallas kernels: 32.7 us -> 30.5 us
    all_to_all x1 -> x0, blocking collectives: 42.1 us -> none  [per_device(): lax.all_to_all(lifted, 'dev', split_axis=0, concat_axis=0, tiled=True)]
    all_to_all x0 -> x1, waiting for transfers between devices: none -> 26.9 us  [per_device(): lax.all_to_all(lifted, 'dev', split_axis=0, concat_axis=0, tiled=True)]
    all_to_all x0 -> x1, starting transfers between devices: none -> 10.6 us  [per_device(): lax.all_to_all(lifted, 'dev', split_axis=0, concat_axis=0, tiled=True)]
    unnamed x14 -> x18, local copies, waits for them, and re-layouts: 0.04 us -> 2.41 us
    pallas_call x1 -> x2, Pallas kernels: 22.7 us -> 20.5 us  [the longest x1 16.4 us: splat(): pl.pallas_call(functools.partial(splat_kernel, groups, 16), out_shape=(ja...]
  transfers between devices with their start and end apart: 2 -> 3, of which waited for: 1 -> 2; matrix products, arithmetic and copies ran while one was open for 1% -> 1% of each run, Pallas kernels for 0% -> 5%
where the time goes in v3:
time: 88.2 us; the launch traced here: 87.9 us
  waiting for transfers between devices  33.8 us (38%)
  Pallas kernels  30.5 us (35%)
  starting transfers between devices  19.9 us (23%)
  local copies, waits for them, and re-layouts  3.12 us (4%)
    all_to_all x1, waiting for transfers between devices, per_device(): lax.all_to_all(lifted, 'dev', split_axis=0, concat_axis=0, tiled=True)  26.9 us
    pallas_call x1, Pallas kernels, splat(): pl.pallas_call(functools.partial(splat_kernel, groups, 16), out_shape=(ja...  16.4 us
    all_to_all x1, starting transfers between devices, per_device(): lax.all_to_all(lifted, 'dev', split_axis=0, concat_axis=0, tiled=True)  10.6 us
    ppermute x1, starting transfers between devices, exchange(): lax.ppermute(bottoms, 'dev', [(i, i + 1) for i in range(devices - 1)])  7.42 us
    ppermute x1, waiting for transfers between devices, exchange(): below = lax.ppermute(tops, 'dev', [(i + 1, i) for i in range(devices - 1)])  6.9 us
    pallas_call x1, Pallas kernels, convolutions(): pl.pallas_call(conv_kernel, out_shape=jax.ShapeDtypeStruct((2, channels,...  5.53 us
    pallas_call x1, Pallas kernels, lift(): pl.pallas_call(functools.partial(lift_kernel, 32), out_shape=jax.ShapeDty...  4.46 us
    pallas_call x1, Pallas kernels, plan(): pl.pallas_call(functools.partial(plan_kernel, 16), out_shape=(jax.ShapeDt...  4.1 us
  transfers between devices with their start and end apart: 3, of which 2 were waited for; matrix products, arithmetic and copies ran while one was open for 1% of the time, Pallas kernels for 5%

profile of v3, /device:TPU:31, one launch (start us, length us, event | category | flops | bytes accessed | tf_op | source)
XLA Modules:
  0.0 87.9 jit_solution(7087057469414166180)
XLA Ops:
  0.0 4.5 %shard_map.100 = bf16[128,80,128]{2,1,0:T(8,128)(2,1)} custom-call(bf16[80,256]{1,0:T(8,128)(2,1)} %context_in.1, bf16[118,256]{1,0:T(8,128)(2,1)} %logits_in.1, s32[128,128]{1,0:T(8,128)} %bitcast.21), custom_call_target="tpu_custom_call" | custom-call | tf_op jit(solution)/shard_map/pallas_call | solution.py:95
  4.5 0.0 copy-start.2
  4.5 10.6 %all-to-all-start = ((bf16[128,80,128]{2,1,0:T(8,128)(2,1)}), bf16[128,80,128]{2,1,0:T(8,128)(2,1)S(1)}, u32[]{:S(2)}, u32[]{:S(2)}) async-start(bf16[128,80,128]{2,1,0:T(8,128)(2,1)} %shard_map.100), calls=%async_computation | async-start | bytes 5242880 | tf_op jit(solution)/shard_map/all_to_all | solution.py:477
  15.0 0.0 copy-done.2
  15.1 0.1 convert_reduce_fusion.1
  15.2 0.3 reduce_window_sum.11
  15.5 0.1 pad.4.starts
  15.6 4.1 %shard_map.101 = (s32[2,128,128]{2,1,0:T(8,128)S(1)}, s32[2,172,128]{2,1,0:T(8,128)S(1)}) custom-call(s32[128,128]{1,0:T(8,128)S(1)} %bitcast.17, s32[2,129]{1,0:T(2,128)S(1)} %pad.4.starts), custom_call_target="tpu_custom_call" | custom-call | flops 1000000000 | bytes 1000000 | tf_op jit(solution)/shard_map/pallas_call | solution.py:190
  19.7 0.0 copy-start.5
  19.7 0.0 copy-start.6
  19.7 0.0 copy-start.7
  19.7 0.0 copy-start.8
  19.7 0.0 copy-start.3
  19.7 26.9 %all-to-all-done.arrived = bf16[128,80,128]{2,1,0:T(8,128)(2,1)S(1)} async-done(((bf16[128,80,128]{2,1,0:T(8,128)(2,1)}), bf16[128,80,128]{2,1,0:T(8,128)(2,1)S(1)}, u32[]{:S(2)}, u32[]{:S(2)}) %all-to-all-start) | async-done | bytes 2621472 | tf_op jit(solution)/shard_map/all_to_all | solution.py:477
  46.6 16.4 %shard_map.102 = (bf16[80,8192]{1,0:T(8,128)(2,1)S(1)}, bf16[80,256]{1,0:T(8,128)(2,1)S(1)}, bf16[80,256]{1,0:T(8,128)(2,1)S(1)}) custom-call(bf16[128,80,128]{2,1,0:T(8,128)(2,1)S(1)} %all-to-all-done.arrived, s32[2,128,128]{2,1,0:T(8,128)S(1)} %get-tuple-element.10.index, s32[2,172,128]{2,1,0:T(8,128)S(1)} %get-tuple-element.11.places, s32[2,129]{1,0:T(2,128)S(1)} %pad.4.starts), custom_call_target="tpu_custom_call" | custom-call | tf_op jit(solution)/shard_map/pallas_call | solution.py:277
  63.0 0.0 copy-start
  63.0 1.0 %copy-done = bf16[80,8192]{1,0:T(8,128)(2,1)} copy-done((bf16[80,8192]{1,0:T(8,128)(2,1)}, bf16[80,8192]{1,0:T(8,128)(2,1)S(1)}, u32[]{:S(2)}) %copy-start) | copy-done | bytes 1310744
  64.1 7.4 %collective-permute-start = (bf16[80,256]{1,0:T(8,128)(2,1)S(1)}, bf16[80,256]{1,0:T(8,128)(2,1)S(1)}, u32[]{:S(2)}, u32[]{:S(2)}) collective-permute-start(bf16[80,256]{1,0:T(8,128)(2,1)S(1)} %get-tuple-element.13), channel_id=1, source_target_pairs={{0,1},{1,2},{2,3},{3,4},{4,5},{5,6},{6,7},{7,8},{8,9},{9,10},{10,1... | collective-permute-start | bytes 122888 | tf_op jit(solution)/shard_map/ppermute | solution.py:454
  71.5 1.9 %collective-permute-start.1 = (bf16[80,256]{1,0:T(8,128)(2,1)S(1)}, bf16[80,256]{1,0:T(8,128)(2,1)S(1)}, u32[]{:S(2)}, u32[]{:S(2)}) collective-permute-start(bf16[80,256]{1,0:T(8,128)(2,1)S(1)} %get-tuple-element.14), channel_id=1, source_target_pairs={{1,0},{2,1},{3,2},{4,3},{5,4},{6,5},{7,6},{8,7},{9,8},{10,9},{11,1... | collective-permute-start | bytes 122888 | tf_op jit(solution)/shard_map/ppermute | solution.py:455
  73.4 0.0 copy-done.4
  73.4 0.2 reshape.12
  73.6 0.0 copy-done.5
  73.6 0.2 reshape.14
  73.8 0.0 copy-done.6
  73.8 0.1 copy.18.scale
  73.9 0.1 copy.19.bias
  74.0 0.0 copy-done.8
  74.0 0.1 copy.20.out_bias
  74.1 0.0 collective-permute-done.above
  74.1 6.9 %collective-permute-done.1.below = bf16[80,256]{1,0:T(8,128)(2,1)S(1)} collective-permute-done((bf16[80,256]{1,0:T(8,128)(2,1)S(1)}, bf16[80,256]{1,0:T(8,128)(2,1)S(1)}, u32[]{:S(2)}, u32[]{:S(2)}) %collective-permute-start.1) | collective-permute-done | bytes 40992 | tf_op jit(solution)/shard_map/ppermute | solution.py:455
  81.0 1.3 %copy-done.1 = bf16[80,8192]{1,0:T(8,128)(2,1)S(1)} copy-done((bf16[80,8192]{1,0:T(8,128)(2,1)S(1)}, bf16[80,8192]{1,0:T(8,128)(2,1)}, u32[]{:S(2)}) %copy-start.1) | copy-done | bytes 1310744
  82.3 5.5 %shard_map.103 = f32[2,80,4096]{2,1,0:T(8,128)} custom-call(bf16[80,8192]{1,0:T(8,128)(2,1)S(1)} %copy-done.1, bf16[80,256]{1,0:T(8,128)(2,1)S(1)} %collective-permute-done.above, bf16[80,256]{1,0:T(8,128)(2,1)S(1)} %collective-permute-done.1.below, s32[2,8]{1,0:T(2,128)S(1)} %bitcast.18, bf16[240,240]{1,0:T(8,128)(2,1)S(1)} %bitcast.15, ...), custom_call_target="tpu_custom_call" | custom-call | tf_op jit(solution)/shard_map/pallas_call | solution.py:436
  (7 shorter events, 0.0 us)
Async XLA Ops:
  4.5 10.6 %copy-start.2 = (s32[1,128,128]{2,1,0:T(8,128)S(1)}, s32[1,128,128]{2,1,0:T(8,128)}, u32[]{:S(2)}) copy-start(s32[1,128,128]{2,1,0:T(8,128)} %param.13) | copy-start | bytes 196612
  4.5 42.1 %all-to-all-start = ((bf16[128,80,128]{2,1,0:T(8,128)(2,1)}), bf16[128,80,128]{2,1,0:T(8,128)(2,1)S(1)}, u32[]{:S(2)}, u32[]{:S(2)}) async-start(bf16[128,80,128]{2,1,0:T(8,128)(2,1)} %shard_map.100), calls=%async_computation | async-start | bytes 5242880 | tf_op jit(solution)/shard_map/all_to_all | solution.py:477
  15.6 57.8 %copy-start.4 = (bf16[80,720]{1,0:T(8,128)(2,1)S(1)}, bf16[80,720]{1,0:T(8,128)(2,1)}, u32[]{:S(2)}) copy-start(bf16[80,720]{1,0:T(8,128)(2,1)} %param.15) | copy-start | bytes 345604
  19.7 53.9 %copy-start.5 = (bf16[80,720]{1,0:T(8,128)(2,1)S(1)}, bf16[80,720]{1,0:T(8,128)(2,1)}, u32[]{:S(2)}) copy-start(bf16[80,720]{1,0:T(8,128)(2,1)} %param.18) | copy-start | bytes 345604
  19.7 54.1 %copy-start.6 = (f32[80]{0:T(128)S(1)}, f32[80]{0:T(128)}, u32[]{:S(2)}) copy-start(f32[80]{0:T(128)} %param.16) | copy-start | bytes 964
  19.7 54.2 %copy-start.7 = (f32[80]{0:T(128)S(1)}, f32[80]{0:T(128)}, u32[]{:S(2)}) copy-start(f32[80]{0:T(128)} %param.17) | copy-start | bytes 964
  19.7 54.3 %copy-start.8 = (f32[80]{0:T(128)S(1)}, f32[80]{0:T(128)}, u32[]{:S(2)}) copy-start(f32[80]{0:T(128)} %param.19) | copy-start | bytes 964
  19.7 61.3 %copy-start.3 = (s32[1,2,8]{2,1,0:T(2,128)S(1)}, s32[1,2,8]{2,1,0:T(2,128)}, u32[]{:S(2)}) copy-start(s32[1,2,8]{2,1,0:T(2,128)} %param.14) | copy-start | bytes 196
  63.0 1.1 %copy-start = (bf16[80,8192]{1,0:T(8,128)(2,1)}, bf16[80,8192]{1,0:T(8,128)(2,1)S(1)}, u32[]{:S(2)}) copy-start(bf16[80,8192]{1,0:T(8,128)(2,1)S(1)} %get-tuple-element.12.field) | copy-start | bytes 3932164
  64.1 10.1 %collective-permute-start = (bf16[80,256]{1,0:T(8,128)(2,1)S(1)}, bf16[80,256]{1,0:T(8,128)(2,1)S(1)}, u32[]{:S(2)}, u32[]{:S(2)}) collective-permute-start(bf16[80,256]{1,0:T(8,128)(2,1)S(1)} %get-tuple-element.13), channel_id=1, source_target_pairs={{0,1},{1,2},{2,3},{3,4},{4,5},{5,6},{6,7},{7,8},{8,9},{9,10},{10,1... | collective-permute-start | bytes 122888 | tf_op jit(solution)/shard_map/ppermute | solution.py:454
  71.5 9.5 %collective-permute-start.1 = (bf16[80,256]{1,0:T(8,128)(2,1)S(1)}, bf16[80,256]{1,0:T(8,128)(2,1)S(1)}, u32[]{:S(2)}, u32[]{:S(2)}) collective-permute-start(bf16[80,256]{1,0:T(8,128)(2,1)S(1)} %get-tuple-element.14), channel_id=1, source_target_pairs={{1,0},{2,1},{3,2},{4,3},{5,4},{6,5},{7,6},{8,7},{9,8},{10,9},{11,1... | collective-permute-start | bytes 122888 | tf_op jit(solution)/shard_map/ppermute | solution.py:455
  81.0 1.3 %copy-start.1 = (bf16[80,8192]{1,0:T(8,128)(2,1)S(1)}, bf16[80,8192]{1,0:T(8,128)(2,1)}, u32[]{:S(2)}) copy-start(bf16[80,8192]{1,0:T(8,128)(2,1)} %copy-done) | copy-start | bytes 3932164

commit v4 on v3

--- a/solution.py
+++ b/solution.py
@@ -202,7 +202,7 @@
 
 
 def splat_kernel(
-    groups, unroll, arrived, index, places, starts, out, tops, bottoms, lists, total, bev, sems
+    groups, unroll, arrived, index, places, starts, bev, tops, bottoms, lists, total
 ):
     sources, channels, slots = arrived.shape
     width = total.shape[2]
@@ -238,7 +238,6 @@
     block = 256
     cell_iota = float_iota((block, span), 0)
     one, zero = jnp.ones((), BF), jnp.zeros((), BF)
-    copies = []
     for n in range(2):
 
         def step(i, carry):
@@ -262,12 +261,7 @@
         for g in range(groups):
             at = slice(n * CELLS + g * width, n * CELLS + (g + 1) * width)
             bev[:, at] = total[n, g * channels : (g + 1) * channels, :].astype(BF)
-        at = slice(n * CELLS, (n + 1) * CELLS)
-        copies.append(pltpu.make_async_copy(bev.at[:, at], out.at[:, at], sems.at[n]))
-        copies[n].start()
     field_edges(bev, tops, bottoms)
-    for copy in copies:
-        copy.wait()
 
 
 def splat(arrived, index, places, starts):
@@ -278,15 +272,39 @@
         functools.partial(splat_kernel, groups, 16),
         out_shape=(jax.ShapeDtypeStruct((channels, 2 * CELLS), BF), edge, edge),
         in_specs=[VMEM, VMEM, VMEM, SMEM],
-        out_specs=(pl.BlockSpec(memory_space=pl.ANY), VMEM, VMEM),
+        out_specs=(VMEM,) * 3,
         scratch_shapes=[
             pltpu.VMEM((2, channels, (sources + 2 * LIST_BLOCK) * slots), BF),
             pltpu.VMEM((2, groups * channels, CELLS // groups), F32),
-            pltpu.VMEM((channels, 2 * CELLS), BF),
-            pltpu.SemaphoreType.DMA((2,)),
         ],
         compiler_params=params(32),
     )(arrived, index, places, starts)
+
+
+def prepare_kernel(conv1, conv2, scale, bias, out_bias, weight1, weight2, vectors, square):
+    channels, taps = scale.shape[1], weight1.shape[0]
+    for source, target in ((conv1, weight1), (conv2, weight2)):
+        for a in range(3):
+            rows = source[:, a * taps : (a + 1) * taps]
+            target[a * channels : (a + 1) * channels, :] = rows
+    square[...] = jnp.zeros(square.shape, F32)
+    for n, vector in enumerate((scale, bias, out_bias)):
+        square[:, 0:channels] = jnp.broadcast_to(vector[...], (square.shape[0], channels))
+        vectors[n] = jnp.transpose(square[...])[0:channels, :]
+
+
+def prepare(conv1, conv2, scale, bias, out_bias):
+    channels = conv1.shape[0]
+    weight = jax.ShapeDtypeStruct((3 * channels, 3 * channels), BF)
+    return pl.pallas_call(
+        prepare_kernel,
+        out_shape=(weight, weight, jax.ShapeDtypeStruct((3, channels, 128), F32)),
+        in_specs=[VMEM] * 5,
+        out_specs=(VMEM,) * 3,
+        scratch_shapes=[pltpu.VMEM((128, 128), F32)],
+        compiler_params=params(16),
+        cost_estimate=pl.CostEstimate(flops=10**8, bytes_accessed=10**6, transcendentals=0),
+    )(conv1, conv2, scale[None], bias[None], out_bias[None])
 
 
 def conv_kernel(
@@ -296,9 +314,7 @@
     links,
     weight1,
     weight2,
-    scale,
-    bias,
-    out_bias,
+    vectors,
     out,
     stack1,
     stack2,
@@ -368,9 +384,7 @@
                 found = jnp.maximum(found, gate(j, a, 0) * gate(j, b, 1))
         return found
 
-    gain = jnp.broadcast_to(scale[...], shape)
-    shift = jnp.broadcast_to(bias[...], shape)
-    last_shift = jnp.broadcast_to(out_bias[...], shape)
+    gain, shift, last_shift = (vectors[n] for n in range(3))
     keep = keeps(gate(1, 3, 0))
     keep_up, keep_down = keeps(joined(0, 1, 2)), keeps(joined(5, 6, 7))
     end = SIDE + 1
@@ -430,13 +444,13 @@
         copy.wait()
 
 
-def convolutions(field, above, below, links, weight1, weight2, scale, bias, out_bias):
+def convolutions(field, above, below, links, weight1, weight2, vectors):
     channels = field.shape[0]
     stack = pltpu.VMEM((3 * channels, (SIDE + 2) * 128), BF)
     return pl.pallas_call(
         conv_kernel,
         out_shape=jax.ShapeDtypeStruct((2, channels, CELLS), F32),
-        in_specs=[VMEM, VMEM, VMEM, SMEM] + [VMEM] * 5,
+        in_specs=[VMEM, VMEM, VMEM, SMEM] + [VMEM] * 3,
         out_specs=pl.BlockSpec(memory_space=pl.ANY),
         scratch_shapes=[
             stack,
@@ -446,7 +460,7 @@
             pltpu.SemaphoreType.DMA((2, 4)),
         ],
         compiler_params=params(44),
-    )(field, above, below, links, weight1, weight2, scale, bias, out_bias)
+    )(field, above, below, links, weight1, weight2, vectors)
 
 
 def exchange(tops, bottoms):
@@ -454,11 +468,6 @@
     above = lax.ppermute(bottoms, "dev", [(i, i + 1) for i in range(devices - 1)])
     below = lax.ppermute(tops, "dev", [(i + 1, i) for i in range(devices - 1)])
     return above, below
-
-
-def by_row_tap(weight):
-    channels = weight.shape[0]
-    return weight.reshape(channels, 3, 3 * channels).transpose(1, 0, 2).reshape(3 * channels, -1)
 
 
 def per_device(
@@ -477,19 +486,11 @@
     arrived = lax.all_to_all(lifted, "dev", split_axis=0, concat_axis=0, tiled=True)
     starts = list_starts(recv_cell[0])
     index, places = plan(recv_cell[0], starts)
+    prepared = prepare(conv1_weight, conv2_weight, layer_scale, layer_bias, out_bias)
+    places, prepared = lax.optimization_barrier((places, prepared))
     bev, tops, bottoms = splat(arrived, index, places, starts)
     above, below = exchange(tops, bottoms)
-    out = convolutions(
-        bev,
-        above,
-        below,
-        neighbour[0],
-        by_row_tap(conv1_weight),
-        by_row_tap(conv2_weight),
-        layer_scale[:, None],
-        layer_bias[:, None],
-        out_bias[:, None],
-    )
+    out = convolutions(bev, above, below, neighbour[0], *prepared)
     return out[None]
 
 

time: 88.2 us -> 85.6 us (0.971)
  local copies, waits for them, and re-layouts: 3.12 us -> 0.12 us
    unnamed x18 -> x14, local copies, waits for them, and re-layouts: 2.41 us -> 0.05 us
where the time goes in v4:
time: 85.6 us; the launch traced here: 85.3 us
  waiting for transfers between devices  34.3 us (40%)
  Pallas kernels  30.4 us (36%)
  starting transfers between devices  19.9 us (23%)
    all_to_all x1, waiting for transfers between devices, per_device(): lax.all_to_all(lifted, 'dev', split_axis=0, concat_axis=0, tiled=True)  26.7 us
    pallas_call x1, Pallas kernels, splat(): pl.pallas_call(functools.partial(splat_kernel, groups, 16), out_shape=(ja...  16.3 us
    all_to_all x1, starting transfers between devices, per_device(): lax.all_to_all(lifted, 'dev', split_axis=0, concat_axis=0, tiled=True)  10.6 us
    ppermute x1, waiting for transfers between devices, exchange(): below = lax.ppermute(tops, 'dev', [(i + 1, i) for i in range(devices - 1)])  7.6 us
    ppermute x1, starting transfers between devices, exchange(): lax.ppermute(bottoms, 'dev', [(i, i + 1) for i in range(devices - 1)])  7.43 us
    pallas_call x1, Pallas kernels, convolutions(): pl.pallas_call(conv_kernel, out_shape=jax.ShapeDtypeStruct((2, channels,...  5.42 us
    pallas_call x1, Pallas kernels, lift(): pl.pallas_call(functools.partial(lift_kernel, 32), out_shape=jax.ShapeDty...  4.46 us
    pallas_call x1, Pallas kernels, plan(): pl.pallas_call(functools.partial(plan_kernel, 16), out_shape=(jax.ShapeDt...  4.09 us
  transfers between devices with their start and end apart: 3, of which 2 were waited for; matrix products, arithmetic and copies ran while one was open for 1% of the time, Pallas kernels for 5%

profile of v4, /device:TPU:31, one launch (start us, length us, event | category | flops | bytes accessed | tf_op | source)
XLA Modules:
  0.0 85.3 jit_solution(12340535807573927036)
XLA Ops:
  0.0 4.5 %shard_map.100 = bf16[128,80,128]{2,1,0:T(8,128)(2,1)} custom-call(bf16[80,256]{1,0:T(8,128)(2,1)} %context_in.1, bf16[118,256]{1,0:T(8,128)(2,1)} %logits_in.1, s32[128,128]{1,0:T(8,128)} %bitcast.16), custom_call_target="tpu_custom_call" | custom-call | tf_op jit(solution)/shard_map/pallas_call | solution.py:95
  4.5 0.0 copy-start
  4.5 0.0 copy-start.2
  4.5 0.0 copy-start.3
  4.5 0.0 copy-start.4
  4.5 0.0 copy-start.5
  4.5 0.0 copy-start.6
  4.5 10.6 %all-to-all-start = ((bf16[128,80,128]{2,1,0:T(8,128)(2,1)}), bf16[128,80,128]{2,1,0:T(8,128)(2,1)S(1)}, u32[]{:S(2)}, u32[]{:S(2)}) async-start(bf16[128,80,128]{2,1,0:T(8,128)(2,1)} %shard_map.100), calls=%async_computation | async-start | bytes 5242880 | tf_op jit(solution)/shard_map/all_to_all | solution.py:486
  15.1 0.0 copy-done
  15.1 0.1 convert_reduce_fusion.1
  15.2 0.3 reduce_window_sum.11
  15.5 0.1 pad.4.starts
  15.6 0.0 copy-done.2
  15.6 0.0 copy-done.3
  15.6 0.0 copy-done.4
  15.6 0.0 copy-done.5
  15.7 0.0 copy-done.6
  15.7 0.2 shard_map.102
  15.9 0.0 copy-start.1
  15.9 4.1 %shard_map.101 = (s32[2,128,128]{2,1,0:T(8,128)S(1)}, s32[2,172,128]{2,1,0:T(8,128)S(1)}) custom-call(s32[128,128]{1,0:T(8,128)S(1)} %bitcast.11, s32[2,129]{1,0:T(2,128)S(1)} %pad.4.starts), custom_call_target="tpu_custom_call" | custom-call | flops 1000000000 | bytes 1000000 | tf_op jit(solution)/shard_map/pallas_call | solution.py:190
  20.0 26.7 %all-to-all-done.arrived = bf16[128,80,128]{2,1,0:T(8,128)(2,1)S(1)} async-done(((bf16[128,80,128]{2,1,0:T(8,128)(2,1)}), bf16[128,80,128]{2,1,0:T(8,128)(2,1)S(1)}, u32[]{:S(2)}, u32[]{:S(2)}) %all-to-all-start) | async-done | bytes 2621472 | tf_op jit(solution)/shard_map/all_to_all | solution.py:486
  46.7 16.3 %shard_map.103 = (bf16[80,8192]{1,0:T(8,128)(2,1)S(1)}, bf16[80,256]{1,0:T(8,128)(2,1)S(1)}, bf16[80,256]{1,0:T(8,128)(2,1)S(1)}) custom-call(bf16[128,80,128]{2,1,0:T(8,128)(2,1)S(1)} %all-to-all-done.arrived, s32[2,128,128]{2,1,0:T(8,128)S(1)} %get-tuple-element.17.index, s32[2,172,128]{2,1,0:T(8,128)S(1)} %get-tuple-element.22.places, s32[2,129]{1,0:T(2,128)S(1)} %pad.4.starts), custom_call_target="tpu_custom_call" | custom-call | tf_op jit(solution)/shard_map/pallas_call | solution.py:271
  62.9 7.4 %collective-permute-start = (bf16[80,256]{1,0:T(8,128)(2,1)S(1)}, bf16[80,256]{1,0:T(8,128)(2,1)S(1)}, u32[]{:S(2)}, u32[]{:S(2)}) collective-permute-start(bf16[80,256]{1,0:T(8,128)(2,1)S(1)} %get-tuple-element.24), channel_id=1, source_target_pairs={{0,1},{1,2},{2,3},{3,4},{4,5},{5,6},{6,7},{7,8},{8,9},{9,10},{10,1... | collective-permute-start | bytes 122888 | tf_op jit(solution)/shard_map/ppermute | solution.py:468
  70.3 1.9 %collective-permute-start.1 = (bf16[80,256]{1,0:T(8,128)(2,1)S(1)}, bf16[80,256]{1,0:T(8,128)(2,1)S(1)}, u32[]{:S(2)}, u32[]{:S(2)}) collective-permute-start(bf16[80,256]{1,0:T(8,128)(2,1)S(1)} %get-tuple-element.25), channel_id=1, source_target_pairs={{1,0},{2,1},{3,2},{4,3},{5,4},{6,5},{7,6},{8,7},{9,8},{10,9},{11,1... | collective-permute-start | bytes 122888 | tf_op jit(solution)/shard_map/ppermute | solution.py:469
  72.3 0.0 collective-permute-done.above
  72.3 7.6 %collective-permute-done.1.below = bf16[80,256]{1,0:T(8,128)(2,1)S(1)} collective-permute-done((bf16[80,256]{1,0:T(8,128)(2,1)S(1)}, bf16[80,256]{1,0:T(8,128)(2,1)S(1)}, u32[]{:S(2)}, u32[]{:S(2)}) %collective-permute-start.1) | collective-permute-done | bytes 40992 | tf_op jit(solution)/shard_map/ppermute | solution.py:469
  79.9 0.0 copy-done.1
  79.9 5.4 %shard_map.104 = f32[2,80,4096]{2,1,0:T(8,128)} custom-call(bf16[80,8192]{1,0:T(8,128)(2,1)S(1)} %get-tuple-element.23.field, bf16[80,256]{1,0:T(8,128)(2,1)S(1)} %collective-permute-done.above, bf16[80,256]{1,0:T(8,128)(2,1)S(1)} %collective-permute-done.1.below, s32[2,8]{1,0:T(2,128)S(1)} %bitcast.12, bf16[240,240]{1,0:T(8,128)(2,1)S(1)} %get-tuple-element.26.weight1, ...), custom_call_target="tpu_custom_call" | custom-call | tf_op jit(solution)/shard_map/pallas_call | solution.py:450
  (1 shorter events, 0.0 us)
Async XLA Ops:
  4.5 10.6 %copy-start = (s32[1,128,128]{2,1,0:T(8,128)S(1)}, s32[1,128,128]{2,1,0:T(8,128)}, u32[]{:S(2)}) copy-start(s32[1,128,128]{2,1,0:T(8,128)} %param.13) | copy-start | bytes 196612
  4.5 11.1 %copy-start.2 = (bf16[80,720]{1,0:T(8,128)(2,1)S(1)}, bf16[80,720]{1,0:T(8,128)(2,1)}, u32[]{:S(2)}) copy-start(bf16[80,720]{1,0:T(8,128)(2,1)} %conv1.1) | copy-start | bytes 345604
  4.5 11.1 %copy-start.3 = (bf16[80,720]{1,0:T(8,128)(2,1)S(1)}, bf16[80,720]{1,0:T(8,128)(2,1)}, u32[]{:S(2)}) copy-start(bf16[80,720]{1,0:T(8,128)(2,1)} %conv2.1) | copy-start | bytes 345604
  4.5 11.1 %copy-start.4 = (f32[80]{0:T(128)S(1)}, f32[80]{0:T(128)}, u32[]{:S(2)}) copy-start(f32[80]{0:T(128)} %param.16) | copy-start | bytes 964
  4.5 11.1 %copy-start.5 = (f32[80]{0:T(128)S(1)}, f32[80]{0:T(128)}, u32[]{:S(2)}) copy-start(f32[80]{0:T(128)} %param.17) | copy-start | bytes 964
  4.5 11.1 %copy-start.6 = (f32[80]{0:T(128)S(1)}, f32[80]{0:T(128)}, u32[]{:S(2)}) copy-start(f32[80]{0:T(128)} %param.19) | copy-start | bytes 964
  4.5 42.1 %all-to-all-start = ((bf16[128,80,128]{2,1,0:T(8,128)(2,1)}), bf16[128,80,128]{2,1,0:T(8,128)(2,1)S(1)}, u32[]{:S(2)}, u32[]{:S(2)}) async-start(bf16[128,80,128]{2,1,0:T(8,128)(2,1)} %shard_map.100), calls=%async_computation | async-start | bytes 5242880 | tf_op jit(solution)/shard_map/all_to_all | solution.py:486
  15.9 64.0 %copy-start.1 = (s32[1,2,8]{2,1,0:T(2,128)S(1)}, s32[1,2,8]{2,1,0:T(2,128)}, u32[]{:S(2)}) copy-start(s32[1,2,8]{2,1,0:T(2,128)} %param.14) | copy-start | bytes 196
  62.9 9.4 %collective-permute-start = (bf16[80,256]{1,0:T(8,128)(2,1)S(1)}, bf16[80,256]{1,0:T(8,128)(2,1)S(1)}, u32[]{:S(2)}, u32[]{:S(2)}) collective-permute-start(bf16[80,256]{1,0:T(8,128)(2,1)S(1)} %get-tuple-element.24), channel_id=1, source_target_pairs={{0,1},{1,2},{2,3},{3,4},{4,5},{5,6},{6,7},{7,8},{8,9},{9,10},{10,1... | collective-permute-start | bytes 122888 | tf_op jit(solution)/shard_map/ppermute | solution.py:468
  70.3 9.5 %collective-permute-start.1 = (bf16[80,256]{1,0:T(8,128)(2,1)S(1)}, bf16[80,256]{1,0:T(8,128)(2,1)S(1)}, u32[]{:S(2)}, u32[]{:S(2)}) collective-permute-start(bf16[80,256]{1,0:T(8,128)(2,1)S(1)} %get-tuple-element.25), channel_id=1, source_target_pairs={{1,0},{2,1},{3,2},{4,3},{5,4},{6,5},{7,6},{8,7},{9,8},{10,9},{11,1... | collective-permute-start | bytes 122888 | tf_op jit(solution)/shard_map/ppermute | solution.py:469

commit v5 on v4

--- a/solution.py
+++ b/solution.py
@@ -9,6 +9,7 @@
 
 SIDE = 64
 CELLS = SIDE * SIDE
+LISTS = 4
 BF = jnp.bfloat16
 F32 = jnp.float32
 VMEM = pl.BlockSpec(memory_space=pltpu.VMEM)
@@ -121,8 +122,8 @@
 
 
 def list_starts(cells):
-    half = (cells >> 11) & 1
-    counts = jnp.stack([jnp.sum((cells >= 0) & (half == n), axis=1, dtype=jnp.int32) for n in range(2)])
+    half = (cells >> 10) & 3
+    counts = jnp.stack([jnp.sum((cells >= 0) & (half == n), axis=1, dtype=jnp.int32) for n in range(LISTS)])
     return jnp.pad(jnp.cumsum(counts, axis=1), ((0, 0), (1, 0)))
 
 
@@ -137,8 +138,8 @@
     after = lax.broadcasted_iota(jnp.int32, (slots, slots), 1)
     earlier = jnp.where(below < after, 1.0, 0.0).astype(BF)
     cell = cells[...]
-    for n in range(2):
-        member = jnp.where((cell >= 0) & (((cell >> 11) & 1) == n), 1.0, 0.0).astype(BF)
+    for n in range(LISTS):
+        member = jnp.where((cell >= 0) & (((cell >> 10) & 3) == n), 1.0, 0.0).astype(BF)
         found = jnp.dot(member, earlier, preferred_element_type=F32)
         ranks[n] = jnp.where(member.astype(F32) > 0.5, found, -1.0).astype(jnp.int32)
         places[n] = jnp.full(places.shape[1:], -1, jnp.int32)
@@ -154,7 +155,7 @@
             place = field_place(cells[pl.ds(s, 1), :]) + 1
             rows = jnp.where(which == 0, lane, jnp.where(which == 1, place >> 6, place & 63))
             picks = []
-            for n in range(2):
+            for n in range(LISTS):
                 rank = ranks[n, pl.ds(s, 1), :]
                 _, offset, _ = start_of(starts, n, s)
                 to = jnp.where(rank < 0, -1, (rank + offset) & 127).astype(F32).astype(BF)
@@ -165,7 +166,7 @@
                 (((1,), (1,)), ((), ())),
                 preferred_element_type=F32,
             ).astype(jnp.int32)
-            for n in range(2):
+            for n in range(LISTS):
                 mine = found[:, n * slots : (n + 1) * slots]
                 block, offset, full = start_of(starts, n, s)
                 index[n, pl.ds(s, 1), :] = mine[0:1]
@@ -176,12 +177,12 @@
         return carry
 
     lax.fori_loop(0, sources // unroll, step, 0)
-    for n in range(2):
+    for n in range(LISTS):
         total = starts[n, sources]
         places[n, pl.ds(total >> 7, 1), :] = jnp.where(lane < (total & 127), current[n : n + 1, :], -1)
 
 
-LIST_BLOCK = 22
+LIST_BLOCK = 18
 
 
 def plan(cells, starts):
@@ -190,12 +191,12 @@
     return pl.pallas_call(
         functools.partial(plan_kernel, 16),
         out_shape=(
-            jax.ShapeDtypeStruct((2, sources, slots), jnp.int32),
-            jax.ShapeDtypeStruct((2, blocks, slots), jnp.int32),
+            jax.ShapeDtypeStruct((LISTS, sources, slots), jnp.int32),
+            jax.ShapeDtypeStruct((LISTS, blocks, slots), jnp.int32),
         ),
         in_specs=[VMEM, SMEM],
         out_specs=(VMEM, VMEM),
-        scratch_shapes=[pltpu.VMEM((2, sources, slots), jnp.int32), pltpu.VMEM((8, slots), jnp.int32)],
+        scratch_shapes=[pltpu.VMEM((LISTS, sources, slots), jnp.int32), pltpu.VMEM((8, slots), jnp.int32)],
         compiler_params=params(16),
         cost_estimate=pl.CostEstimate(flops=10**9, bytes_accessed=10**6, transcendentals=0),
     )(cells, starts)
@@ -218,7 +219,7 @@
         for u in range(unroll):
             s = i * unroll + u
             values = arrived[s].astype(F32)
-            for n in range(2):
+            for n in range(LISTS):
                 block, offset, full = start_of(starts, n, s)
                 source = jnp.broadcast_to(index[n, pl.ds(s, 1), :], values.shape)
                 moved = jnp.take_along_axis(values, source, axis=1, mode="promise_in_bounds")
@@ -227,8 +228,8 @@
                 carry[n] = jnp.where(full, moved, stored)
         return tuple(carry)
 
-    rest = lax.fori_loop(0, sources // unroll, gather, (nothing, nothing))
-    for n in range(2):
+    rest = lax.fori_loop(0, sources // unroll, gather, (nothing,) * LISTS)
+    for n in range(LISTS):
         end = starts[n, sources] >> 7
         put(n, end, rest[n])
         for b in range(1, LIST_BLOCK + 1):
@@ -238,13 +239,13 @@
     block = 256
     cell_iota = float_iota((block, span), 0)
     one, zero = jnp.ones((), BF), jnp.zeros((), BF)
-    for n in range(2):
+    for n in range(LISTS):
 
         def step(i, carry):
             values = lists[n, :, pl.ds(pl.multiple_of(i * span, span), span)]
             rows = [places[n, pl.ds(i * LIST_BLOCK + u, 1), :] for u in range(LIST_BLOCK)]
             target = jnp.concatenate(rows, axis=1)
-            target = jnp.where(target < 0, -1, target - n * CELLS)
+            target = jnp.where(target < 0, -1, target - n * (2 * CELLS // LISTS))
             group = target >> shift
             place = target & (width - 1)
             masked = [values * jnp.where(group == g, 1.0, 0.0).astype(BF) for g in range(groups)]
@@ -259,7 +260,7 @@
 
         lax.fori_loop(0, (starts[n, sources] + span - 1) // span, step, 0)
         for g in range(groups):
-            at = slice(n * CELLS + g * width, n * CELLS + (g + 1) * width)
+            at = slice((n * groups + g) * width, (n * groups + g + 1) * width)
             bev[:, at] = total[n, g * channels : (g + 1) * channels, :].astype(BF)
     field_edges(bev, tops, bottoms)
 
@@ -274,8 +275,8 @@
         in_specs=[VMEM, VMEM, VMEM, SMEM],
         out_specs=(VMEM,) * 3,
         scratch_shapes=[
-            pltpu.VMEM((2, channels, (sources + 2 * LIST_BLOCK) * slots), BF),
-            pltpu.VMEM((2, groups * channels, CELLS // groups), F32),
+            pltpu.VMEM((LISTS, channels, (sources + 2 * LIST_BLOCK) * slots), BF),
+            pltpu.VMEM((LISTS, groups * channels, 2 * CELLS // LISTS // groups), F32),
         ],
         compiler_params=params(32),
     )(arrived, index, places, starts)

time: 85.6 us -> 83.2 us (0.972)
  waiting for transfers between devices: 34.3 us -> 31.4 us
    all_to_all x1, waiting for transfers between devices: 26.7 us -> 23.8 us  [per_device(): lax.all_to_all(lifted, 'dev', split_axis=0, concat_axis=0, tiled=True)]
    pallas_call x1, Pallas kernels: 16.3 us -> 13.9 us  [splat(): pl.pallas_call(functools.partial(splat_kernel, groups, 16), out_shape=(ja...]
    pallas_call x1, Pallas kernels: 4.09 us -> 6.24 us  [plan(): pl.pallas_call(functools.partial(plan_kernel, 16), out_shape=(jax.ShapeDt...]
  transfers between devices with their start and end apart: 3 -> 3, of which waited for: 2 -> 2; matrix products, arithmetic and copies ran while one was open for 1% -> 1% of each run, Pallas kernels for 5% -> 8%
where the time goes in v5:
time: 83.2 us; the launch traced here: 83 us
  waiting for transfers between devices  31.4 us (38%)
  Pallas kernels  30.2 us (36%)
  starting transfers between devices  19.9 us (24%)
    all_to_all x1, waiting for transfers between devices, per_device(): lax.all_to_all(lifted, 'dev', split_axis=0, concat_axis=0, tiled=True)  23.8 us
    pallas_call x1, Pallas kernels, splat(): pl.pallas_call(functools.partial(splat_kernel, groups, 16), out_shape=(ja...  13.9 us
    all_to_all x1, starting transfers between devices, per_device(): lax.all_to_all(lifted, 'dev', split_axis=0, concat_axis=0, tiled=True)  10.6 us
    ppermute x1, waiting for transfers between devices, exchange(): below = lax.ppermute(tops, 'dev', [(i + 1, i) for i in range(devices - 1)])  7.6 us
    ppermute x1, starting transfers between devices, exchange(): lax.ppermute(bottoms, 'dev', [(i, i + 1) for i in range(devices - 1)])  7.42 us
    pallas_call x1, Pallas kernels, plan(): pl.pallas_call(functools.partial(plan_kernel, 16), out_shape=(jax.ShapeDt...  6.24 us
    pallas_call x1, Pallas kernels, convolutions(): pl.pallas_call(conv_kernel, out_shape=jax.ShapeDtypeStruct((2, channels,...  5.41 us
    pallas_call x1, Pallas kernels, lift(): pl.pallas_call(functools.partial(lift_kernel, 32), out_shape=jax.ShapeDty...  4.46 us
  transfers between devices with their start and end apart: 3, of which 2 were waited for; matrix products, arithmetic and copies ran while one was open for 1% of the time, Pallas kernels for 8%

profile of v5, /device:TPU:31, one launch (start us, length us, event | category | flops | bytes accessed | tf_op | source)
XLA Modules:
  0.0 83.0 jit_solution(5628508017670330145)
XLA Ops:
  0.0 4.5 %shard_map.100 = bf16[128,80,128]{2,1,0:T(8,128)(2,1)} custom-call(bf16[80,256]{1,0:T(8,128)(2,1)} %context_in.1, bf16[118,256]{1,0:T(8,128)(2,1)} %logits_in.1, s32[128,128]{1,0:T(8,128)} %bitcast.20), custom_call_target="tpu_custom_call" | custom-call | tf_op jit(solution)/shard_map/pallas_call | solution.py:96
  4.5 0.0 copy-start.2
  4.5 0.0 copy-start.4
  4.5 0.0 copy-start.5
  4.5 0.0 copy-start.6
  4.5 0.0 copy-start.7
  4.5 0.0 copy-start.8
  4.5 10.6 %all-to-all-start = ((bf16[128,80,128]{2,1,0:T(8,128)(2,1)}), bf16[128,80,128]{2,1,0:T(8,128)(2,1)S(1)}, u32[]{:S(2)}, u32[]{:S(2)}) async-start(bf16[128,80,128]{2,1,0:T(8,128)(2,1)} %shard_map.100), calls=%async_computation | async-start | bytes 5242880 | tf_op jit(solution)/shard_map/all_to_all | solution.py:487
  15.1 0.0 copy-done.2
  15.1 0.1 convert_reduce_fusion.3
  15.3 0.3 reduce_window_sum.11
  15.6 0.1 pad.4.starts
  15.7 0.0 copy-done.4
  15.7 0.0 copy-done.5
  15.7 0.0 copy-done.6
  15.7 0.0 copy-done.7
  15.7 0.0 copy-done.8
  15.7 0.2 shard_map.102
  15.9 0.0 copy-start
  15.9 0.6 copy-done
  16.6 0.0 copy-start.3
  16.6 6.2 %shard_map.101 = (s32[4,128,128]{2,1,0:T(8,128)S(1)}, s32[4,164,128]{2,1,0:T(8,128)S(1)}) custom-call(s32[128,128]{1,0:T(8,128)S(1)} %bitcast.15, s32[4,129]{1,0:T(4,128)S(1)} %pad.4.starts), custom_call_target="tpu_custom_call" | custom-call | flops 1000000000 | bytes 1000000 | tf_op jit(solution)/shard_map/pallas_call | solution.py:191
  22.8 23.8 %all-to-all-done.arrived = bf16[128,80,128]{2,1,0:T(8,128)(2,1)S(1)} async-done(((bf16[128,80,128]{2,1,0:T(8,128)(2,1)}), bf16[128,80,128]{2,1,0:T(8,128)(2,1)S(1)}, u32[]{:S(2)}, u32[]{:S(2)}) %all-to-all-start) | async-done | bytes 2621472 | tf_op jit(solution)/shard_map/all_to_all | solution.py:487
  46.7 0.0 copy-start.1
  46.7 13.9 %shard_map.103 = (bf16[80,8192]{1,0:T(8,128)(2,1)S(1)}, bf16[80,256]{1,0:T(8,128)(2,1)S(1)}, bf16[80,256]{1,0:T(8,128)(2,1)S(1)}) custom-call(bf16[128,80,128]{2,1,0:T(8,128)(2,1)S(1)} %all-to-all-done.arrived, s32[4,128,128]{2,1,0:T(8,128)S(1)} %get-tuple-element.17.index, s32[4,164,128]{2,1,0:T(8,128)S(1)} %get-tuple-element.22.places, s32[4,129]{1,0:T(4,128)S(1)} %pad.4.starts), custom_call_target="tpu_custom_call" | custom-call | tf_op jit(solution)/shard_map/pallas_call | solution.py:272
  60.6 7.4 %collective-permute-start = (bf16[80,256]{1,0:T(8,128)(2,1)S(1)}, bf16[80,256]{1,0:T(8,128)(2,1)S(1)}, u32[]{:S(2)}, u32[]{:S(2)}) collective-permute-start(bf16[80,256]{1,0:T(8,128)(2,1)S(1)} %get-tuple-element.24), channel_id=1, source_target_pairs={{0,1},{1,2},{2,3},{3,4},{4,5},{5,6},{6,7},{7,8},{8,9},{9,10},{10,1... | collective-permute-start | bytes 122888 | tf_op jit(solution)/shard_map/ppermute | solution.py:469
  68.0 1.9 %collective-permute-start.1 = (bf16[80,256]{1,0:T(8,128)(2,1)S(1)}, bf16[80,256]{1,0:T(8,128)(2,1)S(1)}, u32[]{:S(2)}, u32[]{:S(2)}) collective-permute-start(bf16[80,256]{1,0:T(8,128)(2,1)S(1)} %get-tuple-element.25), channel_id=1, source_target_pairs={{1,0},{2,1},{3,2},{4,3},{5,4},{6,5},{7,6},{8,7},{9,8},{10,9},{11,1... | collective-permute-start | bytes 122888 | tf_op jit(solution)/shard_map/ppermute | solution.py:470
  69.9 0.0 collective-permute-done.above
  70.0 7.6 %collective-permute-done.1.below = bf16[80,256]{1,0:T(8,128)(2,1)S(1)} collective-permute-done((bf16[80,256]{1,0:T(8,128)(2,1)S(1)}, bf16[80,256]{1,0:T(8,128)(2,1)S(1)}, u32[]{:S(2)}, u32[]{:S(2)}) %collective-permute-start.1) | collective-permute-done | bytes 40992 | tf_op jit(solution)/shard_map/ppermute | solution.py:470
  77.6 0.0 copy-done.3
  77.6 0.0 copy-done.1
  77.6 5.4 %shard_map.104 = f32[2,80,4096]{2,1,0:T(8,128)} custom-call(bf16[80,8192]{1,0:T(8,128)(2,1)S(1)} %get-tuple-element.23.field, bf16[80,256]{1,0:T(8,128)(2,1)S(1)} %collective-permute-done.above, bf16[80,256]{1,0:T(8,128)(2,1)S(1)} %collective-permute-done.1.below, s32[2,8]{1,0:T(2,128)S(1)} %bitcast.16, bf16[240,240]{1,0:T(8,128)(2,1)S(1)} %get-tuple-element.26.weight1, ...), custom_call_target="tpu_custom_call" | custom-call | tf_op jit(solution)/shard_map/pallas_call | solution.py:451
  (1 shorter events, 0.0 us)
Async XLA Ops:
  4.5 10.6 %copy-start.2 = (s32[1,128,128]{2,1,0:T(8,128)S(1)}, s32[1,128,128]{2,1,0:T(8,128)}, u32[]{:S(2)}) copy-start(s32[1,128,128]{2,1,0:T(8,128)} %param.13) | copy-start | bytes 196612
  4.5 11.2 %copy-start.4 = (bf16[80,720]{1,0:T(8,128)(2,1)S(1)}, bf16[80,720]{1,0:T(8,128)(2,1)}, u32[]{:S(2)}) copy-start(bf16[80,720]{1,0:T(8,128)(2,1)} %conv1.1) | copy-start | bytes 345604
  4.5 11.2 %copy-start.5 = (bf16[80,720]{1,0:T(8,128)(2,1)S(1)}, bf16[80,720]{1,0:T(8,128)(2,1)}, u32[]{:S(2)}) copy-start(bf16[80,720]{1,0:T(8,128)(2,1)} %conv2.1) | copy-start | bytes 345604
  4.5 11.2 %copy-start.6 = (f32[80]{0:T(128)S(1)}, f32[80]{0:T(128)}, u32[]{:S(2)}) copy-start(f32[80]{0:T(128)} %param.16) | copy-start | bytes 964
  4.5 11.2 %copy-start.7 = (f32[80]{0:T(128)S(1)}, f32[80]{0:T(128)}, u32[]{:S(2)}) copy-start(f32[80]{0:T(128)} %param.17) | copy-start | bytes 964
  4.5 11.2 %copy-start.8 = (f32[80]{0:T(128)S(1)}, f32[80]{0:T(128)}, u32[]{:S(2)}) copy-start(f32[80]{0:T(128)} %param.19) | copy-start | bytes 964
  4.5 42.1 %all-to-all-start = ((bf16[128,80,128]{2,1,0:T(8,128)(2,1)}), bf16[128,80,128]{2,1,0:T(8,128)(2,1)S(1)}, u32[]{:S(2)}, u32[]{:S(2)}) async-start(bf16[128,80,128]{2,1,0:T(8,128)(2,1)} %shard_map.100), calls=%async_computation | async-start | bytes 5242880 | tf_op jit(solution)/shard_map/all_to_all | solution.py:487
  15.9 0.7 copy-start
  16.6 61.0 %copy-start.3 = (s32[1,2,8]{2,1,0:T(2,128)S(1)}, s32[1,2,8]{2,1,0:T(2,128)}, u32[]{:S(2)}) copy-start(s32[1,2,8]{2,1,0:T(2,128)} %param.14) | copy-start | bytes 196
  46.7 30.9 %copy-start.1 = (f32[3,80,128]{2,1,0:T(8,128)S(1)}, f32[3,80,128]{2,1,0:T(8,128)}, u32[]{:S(2)}) copy-start(f32[3,80,128]{2,1,0:T(8,128)} %copy-done) | copy-start | bytes 368644
  60.6 9.4 %collective-permute-start = (bf16[80,256]{1,0:T(8,128)(2,1)S(1)}, bf16[80,256]{1,0:T(8,128)(2,1)S(1)}, u32[]{:S(2)}, u32[]{:S(2)}) collective-permute-start(bf16[80,256]{1,0:T(8,128)(2,1)S(1)} %get-tuple-element.24), channel_id=1, source_target_pairs={{0,1},{1,2},{2,3},{3,4},{4,5},{5,6},{6,7},{7,8},{8,9},{9,10},{10,1... | collective-permute-start | bytes 122888 | tf_op jit(solution)/shard_map/ppermute | solution.py:469
  68.0 9.5 %collective-permute-start.1 = (bf16[80,256]{1,0:T(8,128)(2,1)S(1)}, bf16[80,256]{1,0:T(8,128)(2,1)S(1)}, u32[]{:S(2)}, u32[]{:S(2)}) collective-permute-start(bf16[80,256]{1,0:T(8,128)(2,1)S(1)} %get-tuple-element.25), channel_id=1, source_target_pairs={{1,0},{2,1},{3,2},{4,3},{5,4},{6,5},{7,6},{8,7},{9,8},{10,9},{11,1... | collective-permute-start | bytes 122888 | tf_op jit(solution)/shard_map/ppermute | solution.py:470

commit v6 on v5

--- a/solution.py
+++ b/solution.py
@@ -182,12 +182,12 @@
         places[n, pl.ds(total >> 7, 1), :] = jnp.where(lane < (total & 127), current[n : n + 1, :], -1)
 
 
-LIST_BLOCK = 18
+LIST_BLOCK = 34
 
 
 def plan(cells, starts):
     sources, slots = cells.shape
-    blocks = sources + 2 * LIST_BLOCK
+    blocks = sources + LIST_BLOCK + 6
     return pl.pallas_call(
         functools.partial(plan_kernel, 16),
         out_shape=(
@@ -270,12 +270,12 @@
     groups = 4
     edge = jax.ShapeDtypeStruct((channels, 256), BF)
     return pl.pallas_call(
-        functools.partial(splat_kernel, groups, 16),
+        functools.partial(splat_kernel, groups, 32),
         out_shape=(jax.ShapeDtypeStruct((channels, 2 * CELLS), BF), edge, edge),
         in_specs=[VMEM, VMEM, VMEM, SMEM],
         out_specs=(VMEM,) * 3,
         scratch_shapes=[
-            pltpu.VMEM((LISTS, channels, (sources + 2 * LIST_BLOCK) * slots), BF),
+            pltpu.VMEM((LISTS, channels, (sources + LIST_BLOCK + 6) * slots), BF),
             pltpu.VMEM((LISTS, groups * channels, 2 * CELLS // LISTS // groups), F32),
         ],
         compiler_params=params(32),

time: 83.2 us -> 82.5 us (level)
  Pallas kernels: 30.2 us -> 29.3 us
    pallas_call x1, Pallas kernels: 13.9 us -> 13 us  [splat(): pl.pallas_call(functools.partial(splat_kernel, groups, 32), out_shape=(ja...]
where the time goes in v6:
time: 82.5 us; the launch traced here: 82.2 us
  waiting for transfers between devices  31.3 us (38%)
  Pallas kernels  29.3 us (36%)
  starting transfers between devices  20.1 us (24%)
    all_to_all x1, waiting for transfers between devices, per_device(): lax.all_to_all(lifted, 'dev', split_axis=0, concat_axis=0, tiled=True)  23.8 us
    pallas_call x1, Pallas kernels, splat(): pl.pallas_call(functools.partial(splat_kernel, groups, 32), out_shape=(ja...  13 us
    all_to_all x1, starting transfers between devices, per_device(): lax.all_to_all(lifted, 'dev', split_axis=0, concat_axis=0, tiled=True)  10.6 us
    ppermute x1, starting transfers between devices, exchange(): lax.ppermute(bottoms, 'dev', [(i, i + 1) for i in range(devices - 1)])  7.44 us
    ppermute x1, waiting for transfers between devices, exchange(): below = lax.ppermute(tops, 'dev', [(i + 1, i) for i in range(devices - 1)])  7.42 us
    pallas_call x1, Pallas kernels, plan(): pl.pallas_call(functools.partial(plan_kernel, 16), out_shape=(jax.ShapeDt...  6.24 us
    pallas_call x1, Pallas kernels, convolutions(): pl.pallas_call(conv_kernel, out_shape=jax.ShapeDtypeStruct((2, channels,...  5.41 us
    pallas_call x1, Pallas kernels, lift(): pl.pallas_call(functools.partial(lift_kernel, 32), out_shape=jax.ShapeDty...  4.46 us
  transfers between devices with their start and end apart: 3, of which 2 were waited for; matrix products, arithmetic and copies ran while one was open for 1% of the time, Pallas kernels for 8%

profile of v6, /device:TPU:31, one launch (start us, length us, event | category | flops | bytes accessed | tf_op | source)
XLA Modules:
  0.0 82.2 jit_solution(3633017465072625001)
XLA Ops:
  0.0 4.5 %shard_map.100 = bf16[128,80,128]{2,1,0:T(8,128)(2,1)} custom-call(bf16[80,256]{1,0:T(8,128)(2,1)} %context_in.1, bf16[118,256]{1,0:T(8,128)(2,1)} %logits_in.1, s32[128,128]{1,0:T(8,128)} %bitcast.20), custom_call_target="tpu_custom_call" | custom-call | tf_op jit(solution)/shard_map/pallas_call | solution.py:96
  4.5 0.0 copy-start.2
  4.5 0.0 copy-start.4
  4.5 0.0 copy-start.5
  4.5 0.0 copy-start.6
  4.5 0.0 copy-start.7
  4.5 0.0 copy-start.8
  4.5 10.6 %all-to-all-start = ((bf16[128,80,128]{2,1,0:T(8,128)(2,1)}), bf16[128,80,128]{2,1,0:T(8,128)(2,1)S(1)}, u32[]{:S(2)}, u32[]{:S(2)}) async-start(bf16[128,80,128]{2,1,0:T(8,128)(2,1)} %shard_map.100), calls=%async_computation | async-start | bytes 5242880 | tf_op jit(solution)/shard_map/all_to_all | solution.py:487
  15.1 0.0 copy-done.2
  15.1 0.1 convert_reduce_fusion.3
  15.3 0.3 reduce_window_sum.11
  15.6 0.1 pad.4.starts
  15.7 0.0 copy-done.4
  15.7 0.0 copy-done.5
  15.7 0.0 copy-done.6
  15.7 0.0 copy-done.7
  15.7 0.0 copy-done.8
  15.7 0.2 shard_map.102
  15.9 0.0 copy-start
  15.9 0.6 copy-done
  16.6 0.0 copy-start.3
  16.6 6.2 %shard_map.101 = (s32[4,128,128]{2,1,0:T(8,128)S(1)}, s32[4,168,128]{2,1,0:T(8,128)S(1)}) custom-call(s32[128,128]{1,0:T(8,128)S(1)} %bitcast.15, s32[4,129]{1,0:T(4,128)S(1)} %pad.4.starts), custom_call_target="tpu_custom_call" | custom-call | flops 1000000000 | bytes 1000000 | tf_op jit(solution)/shard_map/pallas_call | solution.py:191
  22.8 23.8 %all-to-all-done.arrived = bf16[128,80,128]{2,1,0:T(8,128)(2,1)S(1)} async-done(((bf16[128,80,128]{2,1,0:T(8,128)(2,1)}), bf16[128,80,128]{2,1,0:T(8,128)(2,1)S(1)}, u32[]{:S(2)}, u32[]{:S(2)}) %all-to-all-start) | async-done | bytes 2621472 | tf_op jit(solution)/shard_map/all_to_all | solution.py:487
  46.7 0.0 copy-start.1
  46.7 13.0 %shard_map.103 = (bf16[80,8192]{1,0:T(8,128)(2,1)S(1)}, bf16[80,256]{1,0:T(8,128)(2,1)S(1)}, bf16[80,256]{1,0:T(8,128)(2,1)S(1)}) custom-call(bf16[128,80,128]{2,1,0:T(8,128)(2,1)S(1)} %all-to-all-done.arrived, s32[4,128,128]{2,1,0:T(8,128)S(1)} %get-tuple-element.17.index, s32[4,168,128]{2,1,0:T(8,128)S(1)} %get-tuple-element.22.places, s32[4,129]{1,0:T(4,128)S(1)} %pad.4.starts), custom_call_target="tpu_custom_call" | custom-call | tf_op jit(solution)/shard_map/pallas_call | solution.py:272
  59.6 7.4 %collective-permute-start = (bf16[80,256]{1,0:T(8,128)(2,1)S(1)}, bf16[80,256]{1,0:T(8,128)(2,1)S(1)}, u32[]{:S(2)}, u32[]{:S(2)}) collective-permute-start(bf16[80,256]{1,0:T(8,128)(2,1)S(1)} %get-tuple-element.24), channel_id=1, source_target_pairs={{0,1},{1,2},{2,3},{3,4},{4,5},{5,6},{6,7},{7,8},{8,9},{9,10},{10,1... | collective-permute-start | bytes 122888 | tf_op jit(solution)/shard_map/ppermute | solution.py:469
  67.1 2.1 %collective-permute-start.1 = (bf16[80,256]{1,0:T(8,128)(2,1)S(1)}, bf16[80,256]{1,0:T(8,128)(2,1)S(1)}, u32[]{:S(2)}, u32[]{:S(2)}) collective-permute-start(bf16[80,256]{1,0:T(8,128)(2,1)S(1)} %get-tuple-element.25), channel_id=1, source_target_pairs={{1,0},{2,1},{3,2},{4,3},{5,4},{6,5},{7,6},{8,7},{9,8},{10,9},{11,1... | collective-permute-start | bytes 122888 | tf_op jit(solution)/shard_map/ppermute | solution.py:470
  69.2 0.0 collective-permute-done.above
  69.2 7.4 %collective-permute-done.1.below = bf16[80,256]{1,0:T(8,128)(2,1)S(1)} collective-permute-done((bf16[80,256]{1,0:T(8,128)(2,1)S(1)}, bf16[80,256]{1,0:T(8,128)(2,1)S(1)}, u32[]{:S(2)}, u32[]{:S(2)}) %collective-permute-start.1) | collective-permute-done | bytes 40992 | tf_op jit(solution)/shard_map/ppermute | solution.py:470
  76.6 0.0 copy-done.3
  76.6 0.0 copy-done.1
  76.6 5.4 %shard_map.104 = f32[2,80,4096]{2,1,0:T(8,128)} custom-call(bf16[80,8192]{1,0:T(8,128)(2,1)S(1)} %get-tuple-element.23.field, bf16[80,256]{1,0:T(8,128)(2,1)S(1)} %collective-permute-done.above, bf16[80,256]{1,0:T(8,128)(2,1)S(1)} %collective-permute-done.1.below, s32[2,8]{1,0:T(2,128)S(1)} %bitcast.16, bf16[240,240]{1,0:T(8,128)(2,1)S(1)} %get-tuple-element.26.weight1, ...), custom_call_target="tpu_custom_call" | custom-call | tf_op jit(solution)/shard_map/pallas_call | solution.py:451
  (1 shorter events, 0.0 us)
Async XLA Ops:
  4.5 10.6 %copy-start.2 = (s32[1,128,128]{2,1,0:T(8,128)S(1)}, s32[1,128,128]{2,1,0:T(8,128)}, u32[]{:S(2)}) copy-start(s32[1,128,128]{2,1,0:T(8,128)} %param.13) | copy-start | bytes 196612
  4.5 11.2 %copy-start.4 = (bf16[80,720]{1,0:T(8,128)(2,1)S(1)}, bf16[80,720]{1,0:T(8,128)(2,1)}, u32[]{:S(2)}) copy-start(bf16[80,720]{1,0:T(8,128)(2,1)} %conv1.1) | copy-start | bytes 345604
  4.5 11.2 %copy-start.5 = (bf16[80,720]{1,0:T(8,128)(2,1)S(1)}, bf16[80,720]{1,0:T(8,128)(2,1)}, u32[]{:S(2)}) copy-start(bf16[80,720]{1,0:T(8,128)(2,1)} %conv2.1) | copy-start | bytes 345604
  4.5 11.2 %copy-start.6 = (f32[80]{0:T(128)S(1)}, f32[80]{0:T(128)}, u32[]{:S(2)}) copy-start(f32[80]{0:T(128)} %param.16) | copy-start | bytes 964
  4.5 11.2 %copy-start.7 = (f32[80]{0:T(128)S(1)}, f32[80]{0:T(128)}, u32[]{:S(2)}) copy-start(f32[80]{0:T(128)} %param.17) | copy-start | bytes 964
  4.5 11.2 %copy-start.8 = (f32[80]{0:T(128)S(1)}, f32[80]{0:T(128)}, u32[]{:S(2)}) copy-start(f32[80]{0:T(128)} %param.19) | copy-start | bytes 964
  4.5 42.1 %all-to-all-start = ((bf16[128,80,128]{2,1,0:T(8,128)(2,1)}), bf16[128,80,128]{2,1,0:T(8,128)(2,1)S(1)}, u32[]{:S(2)}, u32[]{:S(2)}) async-start(bf16[128,80,128]{2,1,0:T(8,128)(2,1)} %shard_map.100), calls=%async_computation | async-start | bytes 5242880 | tf_op jit(solution)/shard_map/all_to_all | solution.py:487
  15.9 0.7 copy-start
  16.6 60.1 %copy-start.3 = (s32[1,2,8]{2,1,0:T(2,128)S(1)}, s32[1,2,8]{2,1,0:T(2,128)}, u32[]{:S(2)}) copy-start(s32[1,2,8]{2,1,0:T(2,128)} %param.14) | copy-start | bytes 196
  46.7 30.0 %copy-start.1 = (f32[3,80,128]{2,1,0:T(8,128)S(1)}, f32[3,80,128]{2,1,0:T(8,128)}, u32[]{:S(2)}) copy-start(f32[3,80,128]{2,1,0:T(8,128)} %copy-done) | copy-start | bytes 368644
  59.6 9.6 %collective-permute-start = (bf16[80,256]{1,0:T(8,128)(2,1)S(1)}, bf16[80,256]{1,0:T(8,128)(2,1)S(1)}, u32[]{:S(2)}, u32[]{:S(2)}) collective-permute-start(bf16[80,256]{1,0:T(8,128)(2,1)S(1)} %get-tuple-element.24), channel_id=1, source_target_pairs={{0,1},{1,2},{2,3},{3,4},{4,5},{5,6},{6,7},{7,8},{8,9},{9,10},{10,1... | collective-permute-start | bytes 122888 | tf_op jit(solution)/shard_map/ppermute | solution.py:469
  67.1 9.5 %collective-permute-start.1 = (bf16[80,256]{1,0:T(8,128)(2,1)S(1)}, bf16[80,256]{1,0:T(8,128)(2,1)S(1)}, u32[]{:S(2)}, u32[]{:S(2)}) collective-permute-start(bf16[80,256]{1,0:T(8,128)(2,1)S(1)} %get-tuple-element.25), channel_id=1, source_target_pairs={{1,0},{2,1},{3,2},{4,3},{5,4},{6,5},{7,6},{8,7},{9,8},{10,9},{11,1... | collective-permute-start | bytes 122888 | tf_op jit(solution)/shard_map/ppermute | solution.py:470
